TPU v7x, 32 devices: a whole 2x2x4 slice. The times are simulated.
32 devices in a mesh: groups: 2 (over y), section: 4 (over z), tensor: 4 (over x, core).
Axes of the slice: x: 2, y: 2, z: 4, core: 2. Of those that a mesh axis runs over, the one named last changes fastest.
Arguments:
- hidden: bfloat16 [128, 32, 8192], P(('groups', 'section'), None, 'tensor'), parts along dimension 0, may hold values from -6 to 6
- kv_weight: bfloat16 [8192, 2, 1024], P(None, None, 'tensor'), may hold values from -0.0625 to 0.0625
- kv_bias: bfloat16 [2, 1024], P(None, 'tensor'), may hold values from -3 to 3
- prompt_len: int32 [128], P('groups'), parts along dimension 0, may hold values from 1 to 32, as said below
- owner: int32 [128], P('groups'), parts along dimension 0, may hold values from 0 to 3, as said below
- queries: bfloat16 [128, 4, 8192], P(('groups', 'section'), None, 'tensor'), parts along dimension 0, may hold values from -15 to 15
- new_kv: bfloat16 [128, 4, 2, 1024], P(('groups', 'section'), None, None, 'tensor'), parts along dimension 0, may hold values from -15 to 15
- block_table: int32 [128, 2], P(('groups', 'section')), parts along dimension 0, may hold values from 0 to 31, as said below
Outputs:
- kv_pool: bfloat16 [2, 256, 16, 1024], P(None, ('groups', 'section'), None, 'tensor'), parts along dimension 1
- decode_out: bfloat16 [128, 4, 8192], P(('groups', 'section'), None, 'tensor'), parts along dimension 0
There are 2 independent parts, one for each index of `groups`. A program takes and returns all parts, laid end to end along the dimension named above; an argument that names none is the same for every part. Nothing has to cross between parts.
Inputs may be any that keep to these rules, and one draw needn't show every extreme that they name: `prompt_len`: some request has exactly 32. Every owner has exactly 16 requests. The 16 requests of one section index come in runs of 4 consecutive ones with one owner, and the runs of one index have different owners. `block_table`: the 16 rows of one owner's slots hold each of 0 .. 31 exactly once.
All inputs are finite; a program needn't handle non-finite values.
Results may differ from a plain program's by a relative error of at most 0.008.
Values may be sent and summed in bfloat16 or wider, within the bound.
A program may use at most 128 MiB of HBM per device.

v0:
```python
import jax
import jax.numpy as jnp
from jax import lax
from jax.sharding import PartitionSpec as P

HD = 128
BLK = 16
STEPS = 4
QPK = 8


rope_base = 1000000.0


def rotary(key_rows, offset):
    half_dim = key_rows.shape[-1] // 2
    row_count = key_rows.shape[-3]
    positions = (jnp.arange(row_count) + offset).astype(jnp.float32)
    inverse = rope_base ** (-(jnp.arange(half_dim).astype(jnp.float32) * 2.0 / key_rows.shape[-1]))
    angles = positions[:, None] * inverse[None, :]
    cosine = jnp.concatenate([jnp.cos(angles), jnp.cos(angles)], axis=-1)[:, None, :]
    sine_part = jnp.concatenate([jnp.sin(angles), jnp.sin(angles)], axis=-1)[:, None, :]
    turned = jnp.concatenate([-key_rows[..., half_dim:], key_rows[..., :half_dim]], axis=-1)
    return key_rows * cosine + turned * sine_part


def finish(partial_value, kv_bias, offset, lengths, groups):
    span_len = partial_value.shape[1]
    biased = partial_value + kv_bias.astype(jnp.float32).reshape(2, groups, HD)
    rotated = rotary(biased[:, :, 0], offset)
    merged = jnp.stack([rotated, biased[:, :, 1]], axis=2)
    positions = jnp.arange(span_len) + offset
    live_rows = positions[None, :] < lengths[:, None]
    return jnp.where(live_rows[:, :, None, None, None], merged, 0.0).astype(jnp.bfloat16)


def folder(weight_mat):

    def add_slab(running, slab, first_col):
        col_count = slab.shape[-1]
        return jnp.dot(slab.reshape(-1, col_count), weight_mat, preferred_element_type=jnp.float32)

    return add_slab


def attend(query_rows, slot_kv, new_kv, slot_len, groups):
    slot_count = query_rows.shape[0]
    queries = query_rows.reshape(slot_count, STEPS, groups, QPK, HD)
    cached = slot_kv.reshape(slot_count, -1, 2, groups, HD)
    recent = new_kv.reshape(slot_count, STEPS, 2, groups, HD)
    score_scale = HD ** (-0.5)
    old_scores = (
        jnp.einsum(
            "rtgqd,rpgd->rtgqp", queries, cached[:, :, 0], preferred_element_type=jnp.float32
        )
        * score_scale
    )
    new_scores = (
        jnp.einsum(
            "rtgqd,rsgd->rtgqs", queries, recent[:, :, 0], preferred_element_type=jnp.float32
        )
        * score_scale
    )
    prompt_slots = cached.shape[1]
    prompt_pos = jnp.arange(prompt_slots)
    old_live = (prompt_pos[None, :] < slot_len[:, None])[:, None, None, None, :]
    step_pos = jnp.arange(STEPS)
    new_live = (step_pos[None, :] <= step_pos[:, None])[None, :, None, None, :]
    scores = jnp.concatenate(
        [jnp.where(old_live, old_scores, -jnp.inf), jnp.where(new_live, new_scores, -jnp.inf)],
        axis=-1,
    )
    attn_probs = jax.nn.softmax(scores, axis=-1).astype(jnp.bfloat16)
    attended = jnp.einsum(
        "rtgqp,rpgd->rtgqd",
        attn_probs[..., :prompt_slots],
        cached[:, :, 1],
        preferred_element_type=jnp.float32,
    )
    attended = attended + jnp.einsum(
        "rtgqs,rsgd->rtgqd",
        attn_probs[..., prompt_slots:],
        recent[:, :, 1],
        preferred_element_type=jnp.float32,
    )
    return attended.astype(jnp.bfloat16).reshape(slot_count, STEPS, groups * QPK * HD)


def per_device(hidden, kv_weight, kv_bias, prompt_len, owner, queries, new_kv, block_table):
    n_section = lax.axis_size("section")
    own_index = lax.axis_index("section")
    req_count = hidden.shape[0]
    prompt_max = hidden.shape[1]
    kv_width = kv_weight.shape[2]
    groups = kv_width // HD
    run_most = max(2, req_count // n_section)
    owner_grid = owner.reshape(n_section, req_count)
    local_owner = lax.dynamic_index_in_dim(owner_grid, own_index, 0, keepdims=False)
    local_len = lax.dynamic_slice_in_dim(prompt_len, own_index * req_count, req_count)
    local_ids = jnp.arange(req_count)
    earlier = (local_owner[:, None] == local_owner[None, :]) & (
        local_ids[None, :] < local_ids[:, None]
    )
    send_pos = local_owner * run_most + jnp.sum(earlier.astype(jnp.int32), axis=1)
    run_rank = jnp.cumsum((owner_grid == own_index).astype(jnp.int32), axis=1) - 1
    slot_order = jnp.argsort(owner, stable=True)
    own_slots = lax.dynamic_slice_in_dim(slot_order, own_index * req_count, req_count)
    recv_pos = own_slots // req_count * run_most + run_rank.reshape(-1)[own_slots]
    slot_len = prompt_len[own_slots]
    weight_mat = kv_weight.reshape(kv_weight.shape[0], 2 * kv_width)
    add_slab = folder(weight_mat)
    blank_acc = jnp.zeros((req_count * prompt_max, 2 * kv_width), jnp.float32)
    partial_value = add_slab(
        blank_acc, lax.all_gather(hidden, "tensor", axis=2, tiled=True), jnp.int32(0)
    )
    span_len = partial_value.shape[0] // req_count
    shaped = partial_value.reshape(req_count, span_len, 2, groups, HD)
    kv_rows = finish(shaped, kv_bias, 0, local_len, groups).reshape(
        req_count, span_len, 2, kv_width
    )
    blank_buf = jnp.zeros((n_section * run_most,) + kv_rows.shape[1:], kv_rows.dtype)
    arrived = lax.all_to_all(
        blank_buf.at[send_pos].set(kv_rows), "section", split_axis=0, concat_axis=0, tiled=True
    )
    slot_kv = jnp.take(arrived, recv_pos, axis=0)
    decode_out = attend(queries, slot_kv, new_kv, slot_len, groups)
    block_count = prompt_max // BLK
    blocks = slot_kv.reshape(req_count * block_count, BLK, 2, kv_width)
    pool_rows = jnp.zeros_like(blocks).at[block_table.reshape(-1)].set(blocks)
    return (jnp.transpose(pool_rows, (2, 0, 1, 3)), decode_out)


def solution(mesh):
    return jax.shard_map(
        per_device,
        mesh=mesh,
        in_specs=(
            P(("groups", "section"), None, "tensor"),
            P(None, None, "tensor"),
            P(None, "tensor"),
            P("groups"),
            P("groups"),
            P(("groups", "section"), None, "tensor"),
            P(("groups", "section"), None, None, "tensor"),
            P(("groups", "section"), None),
        ),
        out_specs=(
            P(None, ("groups", "section"), None, "tensor"),
            P(("groups", "section"), None, "tensor"),
        ),
        check_vma=False,
    )
```

profile of v0, /device:TPU:0, one launch (start us, length us, event | category | flops | bytes accessed | tf_op | source)
XLA Modules:
  0.0 117.7 jit_solution(10782825466869791353)
XLA Ops:
  7.2 0.7 all-gather.2.cloned.1.call-update
  7.9 8.0 %copy.131 = bf16[1024,8,2,256]{3,1,2,0:T(8,128)(2,1)} copy(bf16[1024,8,2,256]{3,2,1,0:T(2,128)(2,1)} %bitcast.87) | data formatting | bytes 16777216
  15.9 11.7 %copy.98 = bf16[512,8192]{1,0:T(8,128)(2,1)} copy(bf16[512,8192]{0,1:T(8,128)(2,1)} %bitcast.86) | data formatting | bytes 16777216 | tf_op jit(solution)/shard_map/dot_general | solution.py:41
  27.8 2.0 %sort.17 = (s32[64]{0:T(128)}, s32[64]{0:T(128)S(1)}) sort(s32[64]{0:T(128)S(1)} %copy-done.5, s32[64]{0:T(128)S(1)} %iota.59), dimensions={0}, to_apply=%region_0.1 | sort | flops 384 | bytes 1024 | tf_op jit(solution)/shard_map/jit(argsort)/sort | solution.py:106
  30.3 1.2 %fusion.15 = f32[16,2,4,4,8]{4,2,3,1,0:T(4,128)S(1)} fusion(bf16[16,4,2,8,128]{4,3,2,1,0:T(8,128)(2,1)S(1)} %reshape.204, bf16[16,4,1,2,128]{4,3,2,1,0:T(2,128)(2,1)S(1)} %get-tuple-element.25), kind=kOutput, calls=%fused_computation.33 | convolution fusion | flops 1048576 | bytes 311296 | tf_op jit(solution)/shard_map/rtgqd,rsgd->rtgqs/dot_general | solution.py:59
  32.6 38.0 %all-gather.2.cloned.1.call-done = bf16[16,32,8192]{2,1,0:T(8,128)(2,1)} async-done(((bf16[16,32,2048]{2,1,0:T(8,128)(2,1)}), bf16[16,32,8192]{2,1,0:T(8,128)(2,1)}) %all-gather.2.cloned.1.call-update) | async-done | bytes 8388624 | tf_op jit(solution)/shard_map/all_gather | solution.py:114
  70.6 8.3 %fusion.2 = f32[16,32,2,2,128]{4,1,3,2,0:T(8,128)S(1)} fusion(bf16[2,2,128,8192,1]{3,2,1,0,4:T(8,128)(2,1)} %bitcast.88, bf16[16,32,8192]{2,1,0:T(8,128)(2,1)} %all-gather.2.cloned.1.call-done, f32[2,2,128]{2,1,0:T(2,128)S(1)} %reshape.207), kind=kOutput, calls=%fused_computation.7 | convolution fusion | flops 4295229440 | bytes 17827840 | tf_op jit(solution)/shard_map/dot_general | solution.py:41
  79.4 0.4 copy.100
  79.8 0.4 copy.101
  80.3 1.3 %fusion.9 = bf16[16,32,2,256]{3,2,1,0:T(2,128)(2,1)S(1)} fusion(f32[16,32,1,256]{3,2,1,0:T(1,128)S(1)} %bitcast.92, f32[16,32,1,256]{3,2,1,0:T(1,128)S(1)} %bitcast.91, pred[16,32]{1,0:T(8,128)(4,1)S(1)} %iota_compare_fusion.1), kind=kLoop, calls=%fused_computation.16 | loop fusion | flops 1310720 | bytes 1573376 | tf_op jit(solution)/shard_map/convert_element_type | solution.py:34
  81.7 0.9 broadcast_in_dim.90
  82.5 2.6 %scatter_fusion = bf16[16,32,2,256]{3,1,2,0:T(8,128)(2,1)} fusion(bf16[16,32,2,256]{3,1,2,0:T(8,128)(2,1)} %broadcast_in_dim.90, s32[16]{0:T(128)S(1)} %fusion.21, bf16[16,32,2,256]{3,1,2,0:T(8,128)(2,1)S(1)} %copy.102), kind=kCustom, calls=%fused_computation.3 | custom fusion | bytes 1572928 | tf_op jit(solution)/shard_map/scatter | solution.py:123
  85.1 4.6 %all-to-all-start = ((bf16[16,32,2,256]{3,1,2,0:T(8,128)(2,1)}), bf16[16,32,2,256]{3,1,2,0:T(8,128)(2,1)S(1)}, u32[]{:S(2)}, u32[]{:S(2)}) async-start(bf16[16,32,2,256]{3,1,2,0:T(8,128)(2,1)} %scatter_fusion), calls=%async_computation | async-start | bytes 1048576 | tf_op jit(solution)/shard_map/all_to_all | solution.py:122
  89.8 0.7 gather_fusion.2
  90.4 0.7 gather_fusion
  91.2 0.6 copy.111
  92.4 12.2 %all-to-all-done = bf16[16,32,2,256]{3,1,2,0:T(8,128)(2,1)S(1)} async-done(((bf16[16,32,2,256]{3,1,2,0:T(8,128)(2,1)}), bf16[16,32,2,256]{3,1,2,0:T(8,128)(2,1)S(1)}, u32[]{:S(2)}, u32[]{:S(2)}) %all-to-all-start) | async-done | bytes 524320 | tf_op jit(solution)/shard_map/all_to_all | solution.py:122
  104.6 0.6 gather_fusion.1
  105.5 0.4 fusion.25
  105.9 0.6 fusion.18
  106.5 0.5 divide_convert_fusion
  107.5 0.8 reshape.258
  108.5 1.5 %scatter_fusion.1 = bf16[32,16,2,256]{3,1,2,0:T(8,128)(2,1)S(1)} fusion(bf16[32,16,2,256]{3,1,2,0:T(8,128)(2,1)S(1)} %broadcast_in_dim.85, s32[32]{0:T(128)S(1)} %fusion.20, bf16[32,16,2,256]{3,1,2,0:T(8,128)(2,1)S(1)} %copy.104), kind=kCustom, calls=%fused_computation.4 | custom fusion | bytes 1572992 | tf_op jit(solution)/shard_map/scatter | solution.py:129
  110.1 0.8 copy.116
  (60 shorter events, 4.0 us)
Async XLA Ops:
  7.2 63.4 %all-gather.2.cloned.1.call-start = ((), (), s32[]{:S(2)}) async-start(), calls=%async_computation.1 | async-start | bytes 10485760 | tf_op jit(solution)/shard_map/all_gather | solution.py:114
  15.9 11.8 %copy-start.3 = (bf16[2,256]{1,0:T(2,128)(2,1)S(1)}, bf16[2,256]{1,0:T(2,128)(2,1)}, u32[]{:S(2)}) copy-start(bf16[2,256]{1,0:T(2,128)(2,1)} %param.10) | copy-start | bytes 3076
  15.9 11.8 %copy-start.5 = (s32[64]{0:T(128)S(1)}, s32[64]{0:T(128)}, u32[]{:S(2)}) copy-start(s32[64]{0:T(128)} %param.12) | copy-start | bytes 772
  15.9 14.1 %copy-start.1 = (bf16[16,4,2048]{2,1,0:T(4,128)(2,1)S(1)}, bf16[16,4,2048]{2,1,0:T(4,128)(2,1)}, u32[]{:S(2)}) copy-start(bf16[16,4,2048]{2,1,0:T(4,128)(2,1)} %param.13) | copy-start | bytes 786436
  15.9 14.3 %copy-start.2 = (bf16[16,4,2,256]{3,2,1,0:T(2,128)(2,1)S(1)}, bf16[16,4,2,256]{3,2,1,0:T(2,128)(2,1)}, u32[]{:S(2)}) copy-start(bf16[16,4,2,256]{3,2,1,0:T(2,128)(2,1)} %param.14) | copy-start | bytes 196612
  15.9 15.9 %copy-start = (s32[64]{0:T(128)S(1)}, s32[64]{0:T(128)}, u32[]{:S(2)}) copy-start(s32[64]{0:T(128)} %param.11) | copy-start | bytes 772
  78.9 13.2 %copy-start.4 = (s32[16,2]{0,1:T(2,128)S(1)}, s32[16,2]{0,1:T(2,128)}, u32[]{:S(2)}) copy-start(s32[16,2]{0,1:T(2,128)} %param.15) | copy-start | bytes 388
  85.1 19.5 %all-to-all-start = ((bf16[16,32,2,256]{3,1,2,0:T(8,128)(2,1)}), bf16[16,32,2,256]{3,1,2,0:T(8,128)(2,1)S(1)}, u32[]{:S(2)}, u32[]{:S(2)}) async-start(bf16[16,32,2,256]{3,1,2,0:T(8,128)(2,1)} %scatter_fusion), calls=%async_computation | async-start | bytes 1048576 | tf_op jit(solution)/shard_map/all_to_all | solution.py:122
Sparse Core Ops, SparseCore 0:
  9.6 60.9 all-gather.1
where the time goes:
time: 118 us
  waiting for transfers between devices  50.9 us (43%)
  local copies, waits for them, and re-layouts  31.4 us (27%)
  between operations  14.3 us (12%)
  matrix products  10.4 us (9%)
  other arithmetic  6.16 us (5%)
  starting transfers between devices  4.64 us (4%)
    all_gather x1, waiting for transfers between devices, per_device(): lax.all_gather(hidden, 'tensor', axis=2, tiled=True)  38 us
    all_to_all x1, waiting for transfers between devices, per_device(): lax.all_to_all(blank_buf.at[send_pos].set(kv_rows), 'section', split_axis...  12.2 us
    dot_general x1, local copies, waits for them, and re-layouts, add_slab(): jnp.dot(slab.reshape(-1, col_count), weight_mat, preferred_element_type=j...  11.7 us
    unnamed x17, local copies, waits for them, and re-layouts  9.76 us
    dot_general x1, matrix products, add_slab(): jnp.dot(slab.reshape(-1, col_count), weight_mat, preferred_element_type=j...  8.29 us
    all_to_all x1, starting transfers between devices, per_device(): lax.all_to_all(blank_buf.at[send_pos].set(kv_rows), 'section', split_axis...  4.6 us
    scatter x1, local copies, waits for them, and re-layouts, per_device(): blank_buf.at[send_pos].set(kv_rows)  2.56 us
  transfers between devices with their start and end apart: 2, of which 2 were waited for; matrix products, arithmetic and copies ran while one was open for 23% of the time, Pallas kernels for 0%

commit v1 on v0

--- a/solution.py
+++ b/solution.py
@@ -1,6 +1,8 @@
 import jax
 import jax.numpy as jnp
 from jax import lax
+from jax.experimental import pallas as pl
+from jax.experimental.pallas import tpu as pltpu
 from jax.sharding import PartitionSpec as P
 
 HD = 128
@@ -86,7 +88,7 @@
     return attended.astype(jnp.bfloat16).reshape(slot_count, STEPS, groups * QPK * HD)
 
 
-def per_device(hidden, kv_weight, kv_bias, prompt_len, owner, queries, new_kv, block_table):
+def per_device_general(hidden, kv_weight, kv_bias, prompt_len, owner, queries, new_kv, block_table):
     n_section = lax.axis_size("section")
     own_index = lax.axis_index("section")
     req_count = hidden.shape[0]
@@ -129,8 +131,277 @@
     pool_rows = jnp.zeros_like(blocks).at[block_table.reshape(-1)].set(blocks)
     return (jnp.transpose(pool_rows, (2, 0, 1, 3)), decode_out)
 
+MESH = pl.DeviceIdType.MESH
+RUNS = 4
+
+
+def partner_of(me, step):
+    if step == 0:
+        return 3 - me
+    if step == 1:
+        return lax.rem(me + 2, 4)
+    if step == 2:
+        return me + 1 - 2 * lax.rem(me, 2)
+    return me
+
+
+def routed_kernel(
+    h0, h1, h2, h3, x0, w_hbm, bias_ref, cos_ref, sin_ref, live_ref, lencol_ref, inv_ref, q_ref, new_ref,
+    pool_ref, out_ref,
+    gathered, weight, kvbuf, sendbuf,
+    w_sem, own_sem, x0_sem, sib_send, sib_recv, x_send, x_recv, fwd_send, fwd_recv, z_send, z_recv,
+):
+    hidden = (h0, h1, h2, h3)
+    sec = lax.axis_index("section")
+    me = lax.axis_index("tensor")
+    sib = me + 1 - 2 * lax.rem(me, 2)
+    across = lax.rem(me + 2, 4)
+    across_sib = lax.rem(sib + 2, 4)
+    order = (me, sib, across, across_sib)
+    rows = gathered.shape[2]
+
+    barrier = pltpu.get_barrier_semaphore()
+    pl.semaphore_signal(barrier, inc=1, device_id={"tensor": sib}, device_id_type=MESH)
+    pl.semaphore_signal(barrier, inc=1, device_id={"tensor": across}, device_id_type=MESH)
+    for step in range(3):
+        pl.semaphore_signal(
+            barrier, inc=1, device_id={"section": partner_of(sec, step)}, device_id_type=MESH
+        )
+    w_copies = [
+        pltpu.make_async_copy(w_hbm.at[:, t], weight.at[:, t], w_sem.at[i])
+        for i, t in enumerate(order)
+    ]
+    own_copies = [
+        pltpu.make_async_copy(hidden[j], gathered.at[j, me], own_sem.at[j]) for j in range(RUNS)
+    ]
+    x0_copy = pltpu.make_async_copy(x0, gathered.at[0, across], x0_sem)
+    pl.semaphore_wait(barrier, 5)
+
+    def remote(src, dst, send, recv, where):
+        return pltpu.make_async_remote_copy(
+            src_ref=src, dst_ref=dst, send_sem=send, recv_sem=recv, device_id=where, device_id_type=MESH
+        )
+
+    x_copies = [None] + [
+        remote(hidden[j], gathered.at[j, me], x_send.at[j], x_recv.at[j], {"tensor": across})
+        for j in range(1, RUNS)
+    ]
+    sib_copies = [
+        remote(hidden[j], gathered.at[j, me], sib_send.at[j], sib_recv.at[j], {"tensor": sib})
+        for j in range(RUNS)
+    ]
+    fwd_copies = [
+        remote(
+            x0 if j == 0 else gathered.at[j, across],
+            gathered.at[j, across],
+            fwd_send.at[j],
+            fwd_recv.at[j],
+            {"tensor": sib},
+        )
+        for j in range(RUNS)
+    ]
+    x_copies[1].start()
+    sib_copies[0].start()
+    fwd_copies[0].start()
+    x_copies[2].start()
+    w_copies[0].start()
+    own_copies[0].start()
+    w_copies[1].start()
+    x0_copy.start()
+    w_copies[2].start()
+    w_copies[3].start()
+    for j in range(1, RUNS):
+        own_copies[j].start()
+        sib_copies[j].start()
+
+    def half(j, t):
+        a = gathered[j, t]
+        return (
+            jnp.dot(a, weight[0, t], preferred_element_type=jnp.float32),
+            jnp.dot(a, weight[1, t], preferred_element_type=jnp.float32),
+        )
+
+    row = lax.broadcasted_iota(jnp.int32, (128, 128), 0)
+    col = lax.broadcasted_iota(jnp.int32, (128, 128), 1)
+    same_slot = (row // 32) == (col // 32)
+    row16 = lax.broadcasted_iota(jnp.int32, (128, 16), 0)
+    col16 = lax.broadcasted_iota(jnp.int32, (128, 16), 1)
+    new_live = ((row16 // 32) == (col16 // 4)) & ((col16 % 4) <= ((row16 % 32) // 8))
+    contract = (((1,), (1,)), ((), ()))
+
+    def attend_run(s):
+        old_live = same_slot & ((col % 32) < lencol_ref[s])
+        for g in range(2):
+            q = q_ref[g, s]
+            kv = kvbuf[pl.ds(8 * s, 8)].reshape(128, 512)
+            k = kv[:, g * 128 : (g + 1) * 128]
+            v = kv[:, 256 + g * 128 : 256 + (g + 1) * 128]
+            old = lax.dot_general(q, k, contract, preferred_element_type=jnp.float32) * HD ** (-0.5)
+            new = (
+                lax.dot_general(q, new_ref[0, g, s], contract, preferred_element_type=jnp.float32)
+                * HD ** (-0.5)
+            )
+            old = jnp.where(old_live, old, -jnp.inf)
+            new = jnp.where(new_live, new, -jnp.inf)
+            top = jnp.maximum(
+                jnp.max(old, axis=1, keepdims=True), jnp.max(new, axis=1, keepdims=True)
+            )
+            old = jnp.exp(old - top)
+            new = jnp.exp(new - top)
+            total = jnp.sum(old, axis=1, keepdims=True) + jnp.sum(new, axis=1, keepdims=True)
+            old = (old / total).astype(jnp.bfloat16)
+            new = (new / total).astype(jnp.bfloat16)
+            res = jnp.dot(old, v, preferred_element_type=jnp.float32) + jnp.dot(
+                new, new_ref[1, g, s], preferred_element_type=jnp.float32
+            )
+            out_ref[g, s] = res.astype(jnp.bfloat16)
+
+    z_copies = []
+    for j in range(RUNS):
+        if j > 0:
+            x_copies[j].wait_recv()
+            fwd_copies[j].start()
+            if j + 2 < RUNS:
+                x_copies[j + 2].start()
+        own_copies[j].wait()
+        if j == 0:
+            w_copies[0].wait()
+        k_acc, v_acc = half(j, me)
+        sib_copies[j].wait_recv()
+        if j == 0:
+            w_copies[1].wait()
+        k_one, v_one = half(j, sib)
+        k_acc, v_acc = k_acc + k_one, v_acc + v_one
+        if j == 0:
+            x0_copy.wait()
+            w_copies[2].wait()
+        k_one, v_one = half(j, across)
+        k_acc, v_acc = k_acc + k_one, v_acc + v_one
+        fwd_copies[j].wait_recv()
+        if j == 0:
+            w_copies[3].wait()
+        k_one, v_one = half(j, across_sib)
+        k_acc, v_acc = k_acc + k_one, v_acc + v_one
+        k_acc = k_acc + bias_ref[0:1, :]
+        v_acc = v_acc + bias_ref[1:2, :]
+        live = live_ref[j] > 0
+        parts = []
+        for g in range(2):
+            k = k_acc[:, g * 128 : (g + 1) * 128]
+            k = k * cos_ref[...] + pltpu.roll(k, 64, 1) * sin_ref[...]
+            parts.append(jnp.where(live, k, 0.0).astype(jnp.bfloat16))
+        for g in range(2):
+            parts.append(jnp.where(live, v_acc[:, g * 128 : (g + 1) * 128], 0.0).astype(jnp.bfloat16))
+        done = jnp.concatenate(parts, axis=1).reshape(8, 16, 512)
+        if j < RUNS - 1:
+            sendbuf[j] = done
+            copy = remote(
+                sendbuf.at[j],
+                kvbuf.at[pl.ds(8 * sec, 8)],
+                z_send.at[j],
+                z_recv.at[j],
+                {"section": partner_of(sec, j)},
+            )
+            copy.start()
+            z_copies.append(copy)
+        else:
+            kvbuf[pl.ds(8 * sec, 8)] = done
+        if j > 0:
+            z_copies[j - 1].wait_recv()
+            attend_run(partner_of(sec, j - 1))
+    attend_run(sec)
+    for block in range(pool_ref.shape[1]):
+        rows_in = kvbuf[inv_ref[block]]
+        pool_ref[0, block] = rows_in[:, :256]
+        pool_ref[1, block] = rows_in[:, 256:]
+    for j in range(RUNS):
+        sib_copies[j].wait_send()
+        fwd_copies[j].wait_send()
+        if j > 0:
+            x_copies[j].wait_send()
+        if j < RUNS - 1:
+            z_copies[j].wait_send()
+
+
+def per_device_routed(hidden, kv_weight, kv_bias, prompt_len, owner, queries, new_kv, block_table):
+    sec = lax.axis_index("section")
+    req_count, prompt_max, feats = hidden.shape
+    run = req_count // RUNS
+    rows = run * prompt_max
+    run_owner = owner.reshape(-1, RUNS, run)[:, :, 0]
+    run_ids = jnp.arange(RUNS)
+    own_runs = lax.dynamic_index_in_dim(run_owner, sec, 0, keepdims=False)
+    lengths = prompt_len.reshape(-1, RUNS, run)
+    own_len = lax.dynamic_index_in_dim(lengths, sec, 0, keepdims=False)
+    picks = [jnp.sum(jnp.where(own_runs == partner_of(sec, j), run_ids, 0)) for j in range(RUNS)]
+    by_run = hidden.reshape(RUNS, rows, feats)
+    parts = [lax.dynamic_index_in_dim(by_run, pick, 0, keepdims=False) for pick in picks]
+    across = lax.ppermute(parts[0], "tensor", [(t, (t + 2) % 4) for t in range(4)])
+    weight = kv_weight.reshape(4, feats, 2, 256).transpose(2, 0, 1, 3)
+    picked_len = jnp.stack([lax.dynamic_index_in_dim(own_len, p, 0, keepdims=False) for p in picks])
+    positions = jnp.arange(prompt_max)
+    live = (positions[None, None, :] < picked_len[:, :, None]).astype(jnp.float32)
+    live = jnp.broadcast_to(live.reshape(RUNS, rows, 1), (RUNS, rows, HD))
+    mine = (run_owner == sec)[:, :, None]
+    slot_len = jnp.sum(jnp.where(mine, lengths, 0), axis=1)
+    lencol = jnp.repeat(slot_len, prompt_max, axis=1).reshape(-1, 1, rows)
+    table = block_table.reshape(-1)
+    count = table.shape[0]
+    inverse = jnp.sum(
+        jnp.where(table[None, :] == jnp.arange(count)[:, None], jnp.arange(count)[None, :], 0), axis=1
+    ).astype(jnp.int32)
+    freq = rope_base ** (-(jnp.arange(HD // 2).astype(jnp.float32) * 2.0 / HD))
+    angles = positions.astype(jnp.float32)[:, None] * freq[None, :]
+    cosine = jnp.concatenate([jnp.cos(angles), jnp.cos(angles)], axis=-1)
+    sine = jnp.concatenate([-jnp.sin(angles), jnp.sin(angles)], axis=-1)
+    cosine = jnp.tile(cosine, (run, 1))
+    sine = jnp.tile(sine, (run, 1))
+    bias = kv_bias.astype(jnp.float32)
+    q = queries.reshape(4, run, STEPS, 2, QPK, HD).transpose(3, 0, 1, 2, 4, 5).reshape(2, 4, rows, HD)
+    new = new_kv.reshape(4, run, STEPS, 2, 2, HD).transpose(3, 4, 0, 1, 2, 5)
+    new = new.reshape(2, 2, 4, run * STEPS, HD)
+    vmem = pl.BlockSpec(memory_space=pltpu.VMEM)
+    anym = pl.BlockSpec(memory_space=pl.ANY)
+    dma = pltpu.SemaphoreType.DMA
+    pool, out = pl.pallas_call(
+        routed_kernel,
+        out_shape=(
+            jax.ShapeDtypeStruct((2, count, BLK, 256), jnp.bfloat16),
+            jax.ShapeDtypeStruct((2, 4, rows, HD), jnp.bfloat16),
+        ),
+        in_specs=[anym] * 6 + [vmem] * 5 + [pl.BlockSpec(memory_space=pltpu.SMEM)] + [vmem] * 2,
+        out_specs=(vmem, vmem),
+        scratch_shapes=[
+            pltpu.VMEM((RUNS, 4, rows, feats), jnp.bfloat16),
+            pltpu.VMEM((2, 4, feats, 256), jnp.bfloat16),
+            pltpu.VMEM((count, BLK, 512), jnp.bfloat16),
+            pltpu.VMEM((RUNS - 1, 8, BLK, 512), jnp.bfloat16),
+            dma((4,)),
+            dma((RUNS,)),
+            dma,
+            dma((RUNS,)),
+            dma((RUNS,)),
+            dma((RUNS,)),
+            dma((RUNS,)),
+            dma((RUNS,)),
+            dma((RUNS,)),
+            dma((RUNS,)),
+            dma((RUNS,)),
+        ],
+        compiler_params=pltpu.CompilerParams(
+            collective_id=0, has_side_effects=True, vmem_limit_bytes=40 * 1024 * 1024
+        ),
+        cost_estimate=pl.CostEstimate(
+            flops=2 * RUNS * rows * 4 * feats * 512, bytes_accessed=16 * 1024 * 1024, transcendentals=0
+        ),
+    )(*parts, across, weight, bias, cosine, sine, live, lencol, inverse, q, new)
+    out = out.reshape(2, 4, run, STEPS, QPK, HD).transpose(1, 2, 3, 0, 4, 5)
+    return (pool, out.reshape(req_count, STEPS, 2 * QPK * HD))
+
 
 def solution(mesh):
+    routed = mesh.shape["section"] == RUNS and mesh.shape["tensor"] == 4
+    per_device = per_device_routed if routed else per_device_general
     return jax.shard_map(
         per_device,
         mesh=mesh,

time: 118 us -> 76.5 us (0.65)
  the two profiles are of different devices: /device:TPU:0 before, /device:TPU:1 now
where the time goes in v1:
time: 76.5 us; the launch traced here: 76 us
  Pallas kernels  43.3 us (57%)
  local copies, waits for them, and re-layouts  19.3 us (25%)
  between operations  8.43 us (11%)
  other arithmetic  2.8 us (4%)
  starting transfers between devices  2.11 us (3%)
    pallas_call x1, Pallas kernels, per_device_routed(): pl.pallas_call(routed_kernel, out_shape=(jax.ShapeDtypeStruct((2, count,...  43.3 us
    unnamed x5, local copies, waits for them, and re-layouts  12.6 us
    ppermute x1, starting transfers between devices, per_device_routed(): lax.ppermute(parts[0], 'tensor', [(t, (t + 2) % 4) for t in range(4)])  2.11 us
    squeeze x1, local copies, waits for them, and re-layouts, per_device_routed(): lax.dynamic_index_in_dim(by_run, pick, 0, keepdims=False)  1.66 us
  transfers between devices with their start and end apart: 1, of which 0 were waited for; matrix products, arithmetic and copies ran while one was open for 17% of the time, Pallas kernels for 0%

profile of v1, /device:TPU:1, one launch (start us, length us, event | category | flops | bytes accessed | tf_op | source)
XLA Modules:
  0.0 76.0 jit_solution(7511716852254091172)
XLA Ops:
  0.6 0.7 reshape.86
  1.4 0.2 compare_reduce_fusion.1
  1.5 0.6 select_reduce_fusion.2
  4.8 0.7 select_reduce_fusion.4
  10.5 1.7 %dynamic-slice_bitcast_fusion = (bf16[128,2048]{1,0:T(8,128)(2,1)S(1)}, bf16[128,2048]{1,0:T(8,128)(2,1)S(1)}, bf16[128,2048]{1,0:T(8,128)(2,1)S(1)}, bf16[128,2048]{1,0:T(8,128)(2,1)S(1)}) fusion(bf16[4,128,2048]{2,1,0:T(8,128)(2,1)} %bitcast.40, s32[]{:T(128)S(6)} %select_n.62, s32[]{:T(128)S(6)} %select_n.60, s32[]{:T(128)S(6)} %select_n.58, s32[]{:T(128)S(6)} %select_n.56), kind=kLoop, calls=%fused_computation | loop fusion | bytes 4194320 | tf_op jit(solution)/shard_map/jit(dynamic_index_in_dim)/squeeze | solution.py:338
  12.2 2.1 %collective-permute-start = (bf16[128,2048]{1,0:T(8,128)(2,1)S(1)}, bf16[128,2048]{1,0:T(8,128)(2,1)S(1)}, u32[]{:S(2)}, u32[]{:S(2)}) collective-permute-start(bf16[128,2048]{1,0:T(8,128)(2,1)S(1)} %get-tuple-element.13.h0), channel_id=1, source_target_pairs={{0,2},{1,3},{2,0},{3,1},{4,6},{5,7},{6,4},{7,5},{8,10},{9,11},{10,... | collective-permute-start | bytes 1572872 | tf_op jit(solution)/shard_map/ppermute | solution.py:339
  14.3 0.1 compare_reduce_fusion
  14.5 0.7 convert_element_type.36.bias_ref
  15.3 0.7 reshape.88
  16.0 0.1 select_reduce_fusion.1
  16.2 0.1 lt.55
  16.4 0.1 reshape_reshape.3.lencol_ref
  16.5 0.8 %copy.21 = s32[16,2]{1,0:T(8,128)S(1)} copy(s32[16,2]{0,1:T(2,128)} %param.15) | data formatting | bytes 256 | tf_op args[7]
  17.2 0.1 eq.72
  17.3 0.1 select_reduce_fusion.inv_ref
  17.4 0.9 %reshape.91 = bf16[4,4,4,2,2,128]{5,4,3,2,1,0:T(2,128)(2,1)S(1)} reshape(bf16[16,4,2,256]{3,2,1,0:T(2,128)(2,1)} %param.14) | data formatting | bytes 131072 | tf_op jit(solution)/shard_map/reshape | solution.py:361
  18.4 1.1 %reshape.89 = bf16[4,4,4,2,8,128]{5,4,3,2,1,0:T(8,128)(2,1)S(1)} reshape(bf16[16,4,2048]{2,1,0:T(4,128)(2,1)} %param.13) | data formatting | bytes 524288 | tf_op jit(solution)/shard_map/reshape | solution.py:360
  19.5 7.7 %copy.20 = bf16[8192,2,256]{2,0,1:T(8,128)(2,1)} copy(bf16[8192,2,256]{2,1,0:T(2,128)(2,1)} %param.9) | data formatting | bytes 16777216 | tf_op args[1]
  27.2 0.1 fusion
  27.5 0.1 broadcast_in_dim.49.live_ref
  27.6 3.4 %copy-done = bf16[8192,2,256]{2,0,1:T(8,128)(2,1)S(1)} copy-done((bf16[8192,2,256]{2,0,1:T(8,128)(2,1)S(1)}, bf16[8192,2,256]{2,0,1:T(8,128)(2,1)}, u32[]{:S(2)}) %copy-start) | copy-done | bytes 8388632
  31.0 43.3 %shard_map.95 = (bf16[2,32,16,256]{3,2,1,0:T(8,128)(2,1)S(1)}, bf16[2,4,128,128]{3,2,1,0:T(8,128)(2,1)S(1)}) custom-call(bf16[128,2048]{1,0:T(8,128)(2,1)S(1)} %get-tuple-element.13.h0, bf16[128,2048]{1,0:T(8,128)(2,1)S(1)} %get-tuple-element.12.h1, bf16[128,2048]{1,0:T(8,128)(2,1)S(1)} %get-tuple-element.11.h2, bf16[128,2048]{1,0:T(8,128)(2,1)S(1)} %get-tuple-element.10.h3, ...), custom_call_target="tpu_custom_call" | custom-call | flops 4294967296 | bytes 16777216 | tf_op jit(solution)/shard_map/pallas_call | solution.py:366
  74.4 0.8 %reshape.94 = bf16[16,4,2048]{2,1,0:T(4,128)(2,1)} reshape(bf16[4,4,4,2,8,128]{5,4,3,2,1,0:T(8,128)(2,1)S(1)} %copy.24) | data formatting | bytes 524288 | tf_op jit(solution)/shard_map/reshape | solution.py:399
  75.2 0.8 %copy.26 = bf16[2,32,16,256]{3,2,1,0:T(8,128)(2,1)} copy(bf16[2,32,16,256]{3,2,1,0:T(8,128)(2,1)S(1)} %get-tuple-element.29) | data formatting | bytes 1048576
  (17 shorter events, 0.5 us)
Async XLA Ops:
  12.2 15.3 %collective-permute-start = (bf16[128,2048]{1,0:T(8,128)(2,1)S(1)}, bf16[128,2048]{1,0:T(8,128)(2,1)S(1)}, u32[]{:S(2)}, u32[]{:S(2)}) collective-permute-start(bf16[128,2048]{1,0:T(8,128)(2,1)S(1)} %get-tuple-element.13.h0), channel_id=1, source_target_pairs={{0,2},{1,3},{2,0},{3,1},{4,6},{5,7},{6,4},{7,5},{8,10},{9,11},{10,... | collective-permute-start | bytes 1572872 | tf_op jit(solution)/shard_map/ppermute | solution.py:339
  27.6 3.4 %copy-start = (bf16[8192,2,256]{2,0,1:T(8,128)(2,1)S(1)}, bf16[8192,2,256]{2,0,1:T(8,128)(2,1)}, u32[]{:S(2)}) copy-start(bf16[8192,2,256]{2,0,1:T(8,128)(2,1)} %copy.20) | copy-start | bytes 25165828

commit v2 on v1

--- a/solution.py
+++ b/solution.py
@@ -1,3 +1,5 @@
+import functools
+
 import jax
 import jax.numpy as jnp
 from jax import lax
@@ -146,19 +148,18 @@
 
 
 def routed_kernel(
-    h0, h1, h2, h3, x0, w_hbm, bias_ref, cos_ref, sin_ref, live_ref, lencol_ref, inv_ref, q_ref, new_ref,
+    head, h_ref, x0_ref, w_hbm, bias_ref, cos_ref, sin_ref, owner_ref, len_ref, inv_ref, q_ref, new_ref,
     pool_ref, out_ref,
     gathered, weight, kvbuf, sendbuf,
-    w_sem, own_sem, x0_sem, sib_send, sib_recv, x_send, x_recv, fwd_send, fwd_recv, z_send, z_recv,
+    w_sem, sib_send, sib_recv, x_send, x_recv, head_send, head_recv, fwd_send, fwd_recv, z_send, z_recv,
 ):
-    hidden = (h0, h1, h2, h3)
     sec = lax.axis_index("section")
     me = lax.axis_index("tensor")
     sib = me + 1 - 2 * lax.rem(me, 2)
     across = lax.rem(me + 2, 4)
     across_sib = lax.rem(sib + 2, 4)
     order = (me, sib, across, across_sib)
-    rows = gathered.shape[2]
+    rest = gathered.shape[3] - head
 
     barrier = pltpu.get_barrier_semaphore()
     pl.semaphore_signal(barrier, inc=1, device_id={"tensor": sib}, device_id_type=MESH)
@@ -171,48 +172,59 @@
         pltpu.make_async_copy(w_hbm.at[:, t], weight.at[:, t], w_sem.at[i])
         for i, t in enumerate(order)
     ]
-    own_copies = [
-        pltpu.make_async_copy(hidden[j], gathered.at[j, me], own_sem.at[j]) for j in range(RUNS)
-    ]
-    x0_copy = pltpu.make_async_copy(x0, gathered.at[0, across], x0_sem)
-    pl.semaphore_wait(barrier, 5)
+
+    def run_of(source, target):
+        found = jnp.int32(0)
+        for r in range(1, RUNS):
+            found = jnp.where(owner_ref[source * 16 + r * 4] == target, r, found)
+        return found
+
+    runs = [run_of(sec, partner_of(sec, j)) for j in range(RUNS)]
 
     def remote(src, dst, send, recv, where):
         return pltpu.make_async_remote_copy(
             src_ref=src, dst_ref=dst, send_sem=send, recv_sem=recv, device_id=where, device_id_type=MESH
         )
 
-    x_copies = [None] + [
-        remote(hidden[j], gathered.at[j, me], x_send.at[j], x_recv.at[j], {"tensor": across})
-        for j in range(1, RUNS)
+    def same(slot, send, recv, where):
+        return remote(slot, slot, send, recv, where)
+
+    tail = pl.ds(head, rest)
+    x_copies = [
+        same(gathered.at[j, me, :, tail], x_send.at[j], x_recv.at[j], {"tensor": across})
+        for j in range(RUNS)
     ]
     sib_copies = [
-        remote(hidden[j], gathered.at[j, me], sib_send.at[j], sib_recv.at[j], {"tensor": sib})
+        same(gathered.at[j, me], sib_send.at[j], sib_recv.at[j], {"tensor": sib}) for j in range(RUNS)
+    ]
+    head_copies = [
+        same(
+            gathered.at[j, across, :, pl.ds(0, head)], head_send.at[j], head_recv.at[j], {"tensor": sib}
+        )
         for j in range(RUNS)
     ]
     fwd_copies = [
-        remote(
-            x0 if j == 0 else gathered.at[j, across],
-            gathered.at[j, across],
-            fwd_send.at[j],
-            fwd_recv.at[j],
-            {"tensor": sib},
-        )
+        same(gathered.at[j, across, :, tail], fwd_send.at[j], fwd_recv.at[j], {"tensor": sib})
         for j in range(RUNS)
     ]
+    gathered[0, me] = h_ref[runs[0]]
+    pl.semaphore_wait(barrier, 5)
+    x_copies[0].start()
+    gathered[1, me] = h_ref[runs[1]]
     x_copies[1].start()
+    w_copies[0].start()
+    w_copies[1].start()
     sib_copies[0].start()
-    fwd_copies[0].start()
-    x_copies[2].start()
-    w_copies[0].start()
-    own_copies[0].start()
-    w_copies[1].start()
-    x0_copy.start()
+    gathered[0, across, :, 0:head] = x0_ref[runs[0]]
+    head_copies[0].start()
     w_copies[2].start()
     w_copies[3].start()
     for j in range(1, RUNS):
-        own_copies[j].start()
+        if j > 1:
+            gathered[j, me] = h_ref[runs[j]]
         sib_copies[j].start()
+        gathered[j, across, :, 0:head] = x0_ref[runs[j]]
+        head_copies[j].start()
 
     def half(j, t):
         a = gathered[j, t]
@@ -229,8 +241,15 @@
     new_live = ((row16 // 32) == (col16 // 4)) & ((col16 % 4) <= ((row16 % 32) // 8))
     contract = (((1,), (1,)), ((), ()))
 
+    def within(index, source, run):
+        first = source * 16 + run * 4
+        limit = jnp.full(index.shape, len_ref[first], jnp.int32)
+        for i in range(1, 4):
+            limit = jnp.where(index // 32 == i, len_ref[first + i], limit)
+        return (index % 32) < limit
+
     def attend_run(s):
-        old_live = same_slot & ((col % 32) < lencol_ref[s])
+        old_live = same_slot & within(col, s, run_of(s, sec))
         for g in range(2):
             q = q_ref[g, s]
             kv = kvbuf[pl.ds(8 * s, 8)].reshape(128, 512)
@@ -256,14 +275,9 @@
             )
             out_ref[g, s] = res.astype(jnp.bfloat16)
 
+    bias = bias_ref[...].astype(jnp.float32)
     z_copies = []
     for j in range(RUNS):
-        if j > 0:
-            x_copies[j].wait_recv()
-            fwd_copies[j].start()
-            if j + 2 < RUNS:
-                x_copies[j + 2].start()
-        own_copies[j].wait()
         if j == 0:
             w_copies[0].wait()
         k_acc, v_acc = half(j, me)
@@ -272,19 +286,26 @@
             w_copies[1].wait()
         k_one, v_one = half(j, sib)
         k_acc, v_acc = k_acc + k_one, v_acc + v_one
+        if j > 0:
+            z_copies[j - 1].wait_recv()
+            attend_run(partner_of(sec, j - 1))
+        x_copies[j].wait_recv()
+        fwd_copies[j].start()
+        if j + 2 < RUNS:
+            x_copies[j + 2].start()
         if j == 0:
-            x0_copy.wait()
             w_copies[2].wait()
         k_one, v_one = half(j, across)
         k_acc, v_acc = k_acc + k_one, v_acc + v_one
+        head_copies[j].wait_recv()
         fwd_copies[j].wait_recv()
         if j == 0:
             w_copies[3].wait()
         k_one, v_one = half(j, across_sib)
         k_acc, v_acc = k_acc + k_one, v_acc + v_one
-        k_acc = k_acc + bias_ref[0:1, :]
-        v_acc = v_acc + bias_ref[1:2, :]
-        live = live_ref[j] > 0
+        k_acc = k_acc + bias[0:1, :]
+        v_acc = v_acc + bias[1:2, :]
+        live = within(row, sec, runs[j])
         parts = []
         for g in range(2):
             k = k_acc[:, g * 128 : (g + 1) * 128]
@@ -306,9 +327,6 @@
             z_copies.append(copy)
         else:
             kvbuf[pl.ds(8 * sec, 8)] = done
-        if j > 0:
-            z_copies[j - 1].wait_recv()
-            attend_run(partner_of(sec, j - 1))
     attend_run(sec)
     for block in range(pool_ref.shape[1]):
         rows_in = kvbuf[inv_ref[block]]
@@ -316,35 +334,26 @@
         pool_ref[1, block] = rows_in[:, 256:]
     for j in range(RUNS):
         sib_copies[j].wait_send()
+        head_copies[j].wait_send()
         fwd_copies[j].wait_send()
-        if j > 0:
-            x_copies[j].wait_send()
+        x_copies[j].wait_send()
         if j < RUNS - 1:
             z_copies[j].wait_send()
 
 
+HEAD = 512
+
+
 def per_device_routed(hidden, kv_weight, kv_bias, prompt_len, owner, queries, new_kv, block_table):
-    sec = lax.axis_index("section")
     req_count, prompt_max, feats = hidden.shape
     run = req_count // RUNS
     rows = run * prompt_max
-    run_owner = owner.reshape(-1, RUNS, run)[:, :, 0]
-    run_ids = jnp.arange(RUNS)
-    own_runs = lax.dynamic_index_in_dim(run_owner, sec, 0, keepdims=False)
-    lengths = prompt_len.reshape(-1, RUNS, run)
-    own_len = lax.dynamic_index_in_dim(lengths, sec, 0, keepdims=False)
-    picks = [jnp.sum(jnp.where(own_runs == partner_of(sec, j), run_ids, 0)) for j in range(RUNS)]
+    across = lax.ppermute(
+        hidden[:, :, :HEAD].reshape(RUNS, rows, HEAD), "tensor", [(t, (t + 2) % 4) for t in range(4)]
+    )
     by_run = hidden.reshape(RUNS, rows, feats)
-    parts = [lax.dynamic_index_in_dim(by_run, pick, 0, keepdims=False) for pick in picks]
-    across = lax.ppermute(parts[0], "tensor", [(t, (t + 2) % 4) for t in range(4)])
     weight = kv_weight.reshape(4, feats, 2, 256).transpose(2, 0, 1, 3)
-    picked_len = jnp.stack([lax.dynamic_index_in_dim(own_len, p, 0, keepdims=False) for p in picks])
     positions = jnp.arange(prompt_max)
-    live = (positions[None, None, :] < picked_len[:, :, None]).astype(jnp.float32)
-    live = jnp.broadcast_to(live.reshape(RUNS, rows, 1), (RUNS, rows, HD))
-    mine = (run_owner == sec)[:, :, None]
-    slot_len = jnp.sum(jnp.where(mine, lengths, 0), axis=1)
-    lencol = jnp.repeat(slot_len, prompt_max, axis=1).reshape(-1, 1, rows)
     table = block_table.reshape(-1)
     count = table.shape[0]
     inverse = jnp.sum(
@@ -356,45 +365,35 @@
     sine = jnp.concatenate([-jnp.sin(angles), jnp.sin(angles)], axis=-1)
     cosine = jnp.tile(cosine, (run, 1))
     sine = jnp.tile(sine, (run, 1))
-    bias = kv_bias.astype(jnp.float32)
     q = queries.reshape(4, run, STEPS, 2, QPK, HD).transpose(3, 0, 1, 2, 4, 5).reshape(2, 4, rows, HD)
     new = new_kv.reshape(4, run, STEPS, 2, 2, HD).transpose(3, 4, 0, 1, 2, 5)
     new = new.reshape(2, 2, 4, run * STEPS, HD)
     vmem = pl.BlockSpec(memory_space=pltpu.VMEM)
-    anym = pl.BlockSpec(memory_space=pl.ANY)
+    smem = pl.BlockSpec(memory_space=pltpu.SMEM)
+    hbm = pl.BlockSpec(memory_space=pltpu.HBM)
     dma = pltpu.SemaphoreType.DMA
     pool, out = pl.pallas_call(
-        routed_kernel,
+        functools.partial(routed_kernel, HEAD),
         out_shape=(
             jax.ShapeDtypeStruct((2, count, BLK, 256), jnp.bfloat16),
             jax.ShapeDtypeStruct((2, 4, rows, HD), jnp.bfloat16),
         ),
-        in_specs=[anym] * 6 + [vmem] * 5 + [pl.BlockSpec(memory_space=pltpu.SMEM)] + [vmem] * 2,
+        in_specs=[vmem, vmem, hbm, vmem, vmem, vmem, smem, smem, smem, vmem, vmem],
         out_specs=(vmem, vmem),
         scratch_shapes=[
             pltpu.VMEM((RUNS, 4, rows, feats), jnp.bfloat16),
             pltpu.VMEM((2, 4, feats, 256), jnp.bfloat16),
             pltpu.VMEM((count, BLK, 512), jnp.bfloat16),
             pltpu.VMEM((RUNS - 1, 8, BLK, 512), jnp.bfloat16),
-            dma((4,)),
-            dma((RUNS,)),
-            dma,
-            dma((RUNS,)),
-            dma((RUNS,)),
-            dma((RUNS,)),
-            dma((RUNS,)),
-            dma((RUNS,)),
-            dma((RUNS,)),
-            dma((RUNS,)),
-            dma((RUNS,)),
-        ],
+        ]
+        + [dma((4,))] * 11,
         compiler_params=pltpu.CompilerParams(
             collective_id=0, has_side_effects=True, vmem_limit_bytes=40 * 1024 * 1024
         ),
         cost_estimate=pl.CostEstimate(
             flops=2 * RUNS * rows * 4 * feats * 512, bytes_accessed=16 * 1024 * 1024, transcendentals=0
         ),
-    )(*parts, across, weight, bias, cosine, sine, live, lencol, inverse, q, new)
+    )(by_run, across, weight, kv_bias, cosine, sine, owner, prompt_len, inverse, q, new)
     out = out.reshape(2, 4, run, STEPS, QPK, HD).transpose(1, 2, 3, 0, 4, 5)
     return (pool, out.reshape(req_count, STEPS, 2 * QPK * HD))
 

time: 76.5 us -> 66.2 us (0.87)
  the two profiles are of different devices: /device:TPU:1 before, /device:TPU:9 now
where the time goes in v2:
time: 66.2 us; the launch traced here: 65.9 us
  Pallas kernels  46.3 us (70%)
  local copies, waits for them, and re-layouts  16.9 us (26%)
  starting transfers between devices  1.28 us (2%)
  between operations  0.76 us (1%)
    pallas_call x1, Pallas kernels, per_device_routed(): pl.pallas_call(functools.partial(routed_kernel, HEAD), out_shape=(jax.Sha...  46.3 us
    unnamed x13, local copies, waits for them, and re-layouts  12.8 us
  transfers between devices with their start and end apart: 1, of which 1 were waited for; matrix products, arithmetic and copies ran while one was open for 17% of the time, Pallas kernels for 0%

profile of v2, /device:TPU:9, one launch (start us, length us, event | category | flops | bytes accessed | tf_op | source)
XLA Modules:
  0.0 65.9 jit_solution(403317680022473594)
XLA Ops:
  0.6 1.1 %slice.3 = bf16[16,32,512]{2,1,0:T(8,128)(2,1)S(1)} slice(bf16[16,32,2048]{2,1,0:T(8,128)(2,1)} %param.8), slice={[0:16], [0:32], [0:512]} | slice | bytes 1048576 | tf_op jit(solution)/shard_map/slice | solution.py:352
  1.7 1.3 %collective-permute-start = (bf16[4,128,512]{2,1,0:T(8,128)(2,1)S(1)}, bf16[4,128,512]{2,1,0:T(8,128)(2,1)S(1)}, u32[]{:S(2)}, u32[]{:S(2)}) collective-permute-start(bf16[4,128,512]{2,1,0:T(8,128)(2,1)S(1)} %bitcast.25), channel_id=1, source_target_pairs={{0,2},{1,3},{2,0},{3,1},{4,6},{5,7},{6,4},{7,5},{8,10},{9,11},{10,... | collective-permute-start | bytes 1572872 | tf_op jit(solution)/shard_map/ppermute | solution.py:351
  3.0 0.8 %copy.21 = s32[16,2]{1,0:T(8,128)S(1)} copy(s32[16,2]{0,1:T(2,128)} %param.15) | data formatting | bytes 256 | tf_op args[7]
  3.8 0.1 eq.15
  3.8 0.9 %reshape.56 = bf16[4,4,4,2,2,128]{5,4,3,2,1,0:T(2,128)(2,1)S(1)} reshape(bf16[16,4,2,256]{3,2,1,0:T(2,128)(2,1)} %param.14) | data formatting | bytes 131072 | tf_op jit(solution)/shard_map/reshape | solution.py:369
  4.8 1.1 %reshape.54 = bf16[4,4,4,2,8,128]{5,4,3,2,1,0:T(8,128)(2,1)S(1)} reshape(bf16[16,4,2048]{2,1,0:T(4,128)(2,1)} %param.13) | data formatting | bytes 524288 | tf_op jit(solution)/shard_map/reshape | solution.py:368
  5.9 0.0 copy-start.1
  6.0 0.0 copy-start.2
  6.0 0.0 copy-start.3
  6.0 0.0 copy-start.4
  6.0 7.8 %copy.20 = bf16[8192,2,256]{2,0,1:T(8,128)(2,1)} copy(bf16[8192,2,256]{2,1,0:T(2,128)(2,1)} %param.9) | data formatting | bytes 16777216 | tf_op args[1]
  13.8 0.1 select_reduce_fusion.inv_ref
  13.9 0.1 fusion
  14.1 0.1 pad_maximum_fusion
  14.2 0.4 collective-permute-done.x0_ref
  14.6 0.0 copy-done.1
  14.6 0.0 copy-done.2
  14.6 0.0 copy-done.3
  14.6 0.0 copy-done.4
  14.6 3.4 %copy-done = bf16[8192,2,256]{2,0,1:T(8,128)(2,1)S(1)} copy-done((bf16[8192,2,256]{2,0,1:T(8,128)(2,1)S(1)}, bf16[8192,2,256]{2,0,1:T(8,128)(2,1)}, u32[]{:S(2)}) %copy-start) | copy-done | bytes 8388632
  18.0 46.3 %shard_map.95 = (bf16[2,32,16,256]{3,2,1,0:T(8,128)(2,1)S(1)}, bf16[2,4,128,128]{3,2,1,0:T(8,128)(2,1)S(1)}) custom-call(bf16[4,128,2048]{2,1,0:T(8,128)(2,1)S(1)} %bitcast.21, bf16[4,128,512]{2,1,0:T(8,128)(2,1)S(1)} %collective-permute-done.x0_ref, bf16[2,4,2048,256]{3,2,1,0:T(8,128)(2,1)S(1)} %bitcast.18, bf16[2,256]{1,0:T(2,128)(2,1)S(1)} %copy-done.2, ...), custom_call_target="tpu_custom_call" | custom-call | flops 4294967296 | bytes 16777216 | tf_op jit(solution)/shard_map/pallas_call | solution.py:375
  64.3 0.1 copy.24
  64.4 0.8 %reshape.59 = bf16[16,4,2048]{2,1,0:T(4,128)(2,1)} reshape(bf16[4,4,4,2,8,128]{5,4,3,2,1,0:T(8,128)(2,1)S(1)} %copy.24) | data formatting | bytes 524288 | tf_op jit(solution)/shard_map/reshape | solution.py:398
  65.1 0.8 %copy.26 = bf16[2,32,16,256]{3,2,1,0:T(8,128)(2,1)} copy(bf16[2,32,16,256]{3,2,1,0:T(8,128)(2,1)S(1)} %get-tuple-element.13) | data formatting | bytes 1048576
  (7 shorter events, 0.1 us)
Async XLA Ops:
  1.7 12.9 %collective-permute-start = (bf16[4,128,512]{2,1,0:T(8,128)(2,1)S(1)}, bf16[4,128,512]{2,1,0:T(8,128)(2,1)S(1)}, u32[]{:S(2)}, u32[]{:S(2)}) collective-permute-start(bf16[4,128,512]{2,1,0:T(8,128)(2,1)S(1)} %bitcast.25), channel_id=1, source_target_pairs={{0,2},{1,3},{2,0},{3,1},{4,6},{5,7},{6,4},{7,5},{8,10},{9,11},{10,... | collective-permute-start | bytes 1572872 | tf_op jit(solution)/shard_map/ppermute | solution.py:351
  5.9 8.6 %copy-start.1 = (bf16[16,32,2048]{2,1,0:T(8,128)(2,1)S(1)}, bf16[16,32,2048]{2,1,0:T(8,128)(2,1)}, u32[]{:S(2)}) copy-start(bf16[16,32,2048]{2,1,0:T(8,128)(2,1)} %param.8) | copy-start | bytes 6291460
  6.0 8.6 %copy-start.2 = (bf16[2,256]{1,0:T(2,128)(2,1)S(1)}, bf16[2,256]{1,0:T(2,128)(2,1)}, u32[]{:S(2)}) copy-start(bf16[2,256]{1,0:T(2,128)(2,1)} %bias_ref.1) | copy-start | bytes 3076
  6.0 8.6 %copy-start.3 = (s32[64]{0:T(128)S(1)}, s32[64]{0:T(128)}, u32[]{:S(2)}) copy-start(s32[64]{0:T(128)} %owner_ref.1) | copy-start | bytes 772
  6.0 8.6 %copy-start.4 = (s32[64]{0:T(128)S(1)}, s32[64]{0:T(128)}, u32[]{:S(2)}) copy-start(s32[64]{0:T(128)} %len_ref.1) | copy-start | bytes 772
  14.6 3.4 %copy-start = (bf16[8192,2,256]{2,0,1:T(8,128)(2,1)S(1)}, bf16[8192,2,256]{2,0,1:T(8,128)(2,1)}, u32[]{:S(2)}) copy-start(bf16[8192,2,256]{2,0,1:T(8,128)(2,1)} %copy.20) | copy-start | bytes 25165828

commit v3 on v2

--- a/solution.py
+++ b/solution.py
@@ -189,9 +189,19 @@
     def same(slot, send, recv, where):
         return remote(slot, slot, send, recv, where)
 
-    tail = pl.ds(head, rest)
+    cut_a, cut_b = rest // 2, rest // 3
+    cuts = [[(j, head, rest)] for j in range(RUNS - 1)]
+    cuts.append([(3, head, cut_a), (4, head + cut_a, cut_b), (5, head + cut_a + cut_b, rest - cut_a - cut_b)])
     x_copies = [
-        same(gathered.at[j, me, :, tail], x_send.at[j], x_recv.at[j], {"tensor": across})
+        [
+            same(
+                gathered.at[j, me, :, pl.ds(first, width)],
+                x_send.at[i],
+                x_recv.at[i],
+                {"tensor": across},
+            )
+            for i, first, width in cuts[j]
+        ]
         for j in range(RUNS)
     ]
     sib_copies = [
@@ -204,14 +214,22 @@
         for j in range(RUNS)
     ]
     fwd_copies = [
-        same(gathered.at[j, across, :, tail], fwd_send.at[j], fwd_recv.at[j], {"tensor": sib})
+        [
+            same(
+                gathered.at[j, across, :, pl.ds(first, width)],
+                fwd_send.at[i],
+                fwd_recv.at[i],
+                {"tensor": sib},
+            )
+            for i, first, width in cuts[j]
+        ]
         for j in range(RUNS)
     ]
     gathered[0, me] = h_ref[runs[0]]
     pl.semaphore_wait(barrier, 5)
-    x_copies[0].start()
+    x_copies[0][0].start()
     gathered[1, me] = h_ref[runs[1]]
-    x_copies[1].start()
+    x_copies[1][0].start()
     w_copies[0].start()
     w_copies[1].start()
     sib_copies[0].start()
@@ -226,11 +244,12 @@
         gathered[j, across, :, 0:head] = x0_ref[runs[j]]
         head_copies[j].start()
 
-    def half(j, t):
-        a = gathered[j, t]
+    def half(j, t, first=0, width=None):
+        span = pl.ds(first, gathered.shape[3] if width is None else width)
+        a = gathered[j, t, :, span]
         return (
-            jnp.dot(a, weight[0, t], preferred_element_type=jnp.float32),
-            jnp.dot(a, weight[1, t], preferred_element_type=jnp.float32),
+            jnp.dot(a, weight[0, t, span], preferred_element_type=jnp.float32),
+            jnp.dot(a, weight[1, t, span], preferred_element_type=jnp.float32),
         )
 
     row = lax.broadcasted_iota(jnp.int32, (128, 128), 0)
@@ -289,20 +308,24 @@
         if j > 0:
             z_copies[j - 1].wait_recv()
             attend_run(partner_of(sec, j - 1))
-        x_copies[j].wait_recv()
-        fwd_copies[j].start()
-        if j + 2 < RUNS:
-            x_copies[j + 2].start()
         if j == 0:
             w_copies[2].wait()
-        k_one, v_one = half(j, across)
-        k_acc, v_acc = k_acc + k_one, v_acc + v_one
+            w_copies[3].wait()
         head_copies[j].wait_recv()
-        fwd_copies[j].wait_recv()
-        if j == 0:
-            w_copies[3].wait()
-        k_one, v_one = half(j, across_sib)
-        k_acc, v_acc = k_acc + k_one, v_acc + v_one
+        for t in (across, across_sib):
+            k_one, v_one = half(j, t, 0, head)
+            k_acc, v_acc = k_acc + k_one, v_acc + v_one
+        for at, (_, first, width) in enumerate(cuts[j]):
+            x_copies[j][at].wait_recv()
+            fwd_copies[j][at].start()
+            if j + 2 < RUNS:
+                for copy in x_copies[j + 2]:
+                    copy.start()
+            k_one, v_one = half(j, across, first, width)
+            k_acc, v_acc = k_acc + k_one, v_acc + v_one
+            fwd_copies[j][at].wait_recv()
+            k_one, v_one = half(j, across_sib, first, width)
+            k_acc, v_acc = k_acc + k_one, v_acc + v_one
         k_acc = k_acc + bias[0:1, :]
         v_acc = v_acc + bias[1:2, :]
         live = within(row, sec, runs[j])
@@ -335,8 +358,9 @@
     for j in range(RUNS):
         sib_copies[j].wait_send()
         head_copies[j].wait_send()
-        fwd_copies[j].wait_send()
-        x_copies[j].wait_send()
+        for at in range(len(cuts[j])):
+            fwd_copies[j][at].wait_send()
+            x_copies[j][at].wait_send()
         if j < RUNS - 1:
             z_copies[j].wait_send()
 
@@ -386,9 +410,9 @@
             pltpu.VMEM((count, BLK, 512), jnp.bfloat16),
             pltpu.VMEM((RUNS - 1, 8, BLK, 512), jnp.bfloat16),
         ]
-        + [dma((4,))] * 11,
+        + [dma((6,))] * 11,
         compiler_params=pltpu.CompilerParams(
-            collective_id=0, has_side_effects=True, vmem_limit_bytes=40 * 1024 * 1024
+            collective_id=0, has_side_effects=True, vmem_limit_bytes=57 * 1024 * 1024
         ),
         cost_estimate=pl.CostEstimate(
             flops=2 * RUNS * rows * 4 * feats * 512, bytes_accessed=16 * 1024 * 1024, transcendentals=0

time: 66.2 us -> 71.1 us (1.074)
  Pallas kernels: 46.3 us -> 49.9 us
  local copies, waits for them, and re-layouts: 16.9 us -> 18 us
    pallas_call x1, Pallas kernels: 46.3 us -> 49.9 us  [per_device_routed(): pl.pallas_call(functools.partial(routed_kernel, HEAD), out_shape=(jax.Sha...]
    unnamed x13 -> x5, local copies, waits for them, and re-layouts: 12.8 us -> 10.3 us
    transpose x1, local copies, waits for them, and re-layouts: 0.06 us -> 1 us  [per_device_routed(): out = out.reshape(2, 4, run, STEPS, QPK, HD).transpose(1, 2, 3, 0, 4, 5)]
  transfers between devices with their start and end apart: 1 -> 1, of which waited for: 1 -> 0; matrix products, arithmetic and copies ran while one was open for 17% -> 18% of each run, Pallas kernels for 0% -> 0%
where the time goes in v3:
time: 71.1 us; the launch traced here: 70.7 us
  Pallas kernels  49.9 us (70%)
  local copies, waits for them, and re-layouts  18 us (25%)
  starting transfers between devices  1.28 us (2%)
  other arithmetic  0.91 us (1%)
    pallas_call x1, Pallas kernels, per_device_routed(): pl.pallas_call(functools.partial(routed_kernel, HEAD), out_shape=(jax.Sha...  49.9 us
    unnamed x5, local copies, waits for them, and re-layouts  10.3 us
    reshape x2, local copies, waits for them, and re-layouts, per_device_routed(): queries.reshape(4, run, STEPS, 2, QPK, HD).transpose(3, 0, 1, 2, 4, 5)  1.87 us
    reshape x2, local copies, waits for them, and re-layouts, per_device_routed(): new = new_kv.reshape(4, run, STEPS, 2, 2, HD).transpose(3, 4, 0, 1, 2, 5)  1.55 us
  transfers between devices with their start and end apart: 1, of which 0 were waited for; matrix products, arithmetic and copies ran while one was open for 18% of the time, Pallas kernels for 0%

profile of v3, /device:TPU:9, one launch (start us, length us, event | category | flops | bytes accessed | tf_op | source)
XLA Modules:
  0.0 70.7 jit_solution(8534473398017347596)
XLA Ops:
  0.6 1.1 %slice.3 = bf16[16,32,512]{2,1,0:T(8,128)(2,1)S(1)} slice(bf16[16,32,2048]{2,1,0:T(8,128)(2,1)} %param.8), slice={[0:16], [0:32], [0:512]} | slice | bytes 1048576 | tf_op jit(solution)/shard_map/slice | solution.py:376
  1.7 1.3 %collective-permute-start = (bf16[4,128,512]{2,1,0:T(8,128)(2,1)S(1)}, bf16[4,128,512]{2,1,0:T(8,128)(2,1)S(1)}, u32[]{:S(2)}, u32[]{:S(2)}) collective-permute-start(bf16[4,128,512]{2,1,0:T(8,128)(2,1)S(1)} %bitcast.19), channel_id=1, source_target_pairs={{0,2},{1,3},{2,0},{3,1},{4,6},{5,7},{6,4},{7,5},{8,10},{9,11},{10,... | collective-permute-start | bytes 1572872 | tf_op jit(solution)/shard_map/ppermute | solution.py:375
  3.0 0.8 %copy.21 = s32[16,2]{1,0:T(8,128)S(1)} copy(s32[16,2]{0,1:T(2,128)} %param.15) | data formatting | bytes 256 | tf_op args[7]
  3.8 0.1 eq.15
  3.8 0.9 %reshape.56 = bf16[4,4,4,2,2,128]{5,4,3,2,1,0:T(2,128)(2,1)S(1)} reshape(bf16[16,4,2,256]{3,2,1,0:T(2,128)(2,1)} %param.14) | data formatting | bytes 131072 | tf_op jit(solution)/shard_map/reshape | solution.py:393
  4.7 0.7 copy.23
  5.4 1.1 %reshape.54 = bf16[4,4,4,2,8,128]{5,4,3,2,1,0:T(8,128)(2,1)S(1)} reshape(bf16[16,4,2048]{2,1,0:T(4,128)(2,1)} %param.13) | data formatting | bytes 524288 | tf_op jit(solution)/shard_map/reshape | solution.py:392
  6.5 0.8 %copy.22 = bf16[4,4,4,2,8,128]{5,4,2,1,0,3:T(8,128)(2,1)} copy(bf16[4,4,4,2,8,128]{5,4,3,2,1,0:T(8,128)(2,1)S(1)} %reshape.54) | data formatting | bytes 524288 | tf_op jit(solution)/shard_map/reshape | solution.py:392
  7.3 7.7 %copy.20 = bf16[8192,2,256]{2,0,1:T(8,128)(2,1)} copy(bf16[8192,2,256]{2,1,0:T(2,128)(2,1)} %param.9) | data formatting | bytes 16777216 | tf_op args[1]
  15.0 0.7 select_reduce_fusion.inv_ref
  15.6 0.1 fusion
  15.8 0.1 pad_maximum_fusion
  15.9 0.0 collective-permute-done.x0_ref
  15.9 0.0 copy-start
  15.9 0.7 tile.8
  16.6 0.6 tile.20
  17.2 0.0 copy-done
  17.2 49.9 %shard_map.95 = (bf16[2,32,16,256]{3,2,1,0:T(8,128)(2,1)}, bf16[2,4,128,128]{3,2,1,0:T(8,128)(2,1)}) custom-call(bf16[4,128,2048]{2,1,0:T(8,128)(2,1)} %bitcast.22, bf16[4,128,512]{2,1,0:T(8,128)(2,1)} %copy-done, bf16[2,4,2048,256]{3,2,1,0:T(8,128)(2,1)} %bitcast.18, bf16[2,256]{1,0:T(2,128)(2,1)} %bias_ref.1, f32[128,128]{1,0:T(8,128)} %bitcast.23, ...), custom_call_target="tpu_custom_call" | custom-call | flops 4294967296 | bytes 16777216 | tf_op jit(solution)/shard_map/pallas_call | solution.py:399
  67.1 1.0 %copy.24 = bf16[4,4,4,2,8,128]{5,4,3,2,1,0:T(8,128)(2,1)S(1)} copy(bf16[4,4,4,2,8,128]{5,4,2,1,0,3:T(8,128)(2,1)} %bitcast.21) | data formatting | bytes 524288 | tf_op jit(solution)/shard_map/transpose | solution.py:421
  68.1 0.8 %reshape.59 = bf16[16,4,2048]{2,1,0:T(4,128)(2,1)} reshape(bf16[4,4,4,2,8,128]{5,4,3,2,1,0:T(8,128)(2,1)S(1)} %copy.24) | data formatting | bytes 524288 | tf_op jit(solution)/shard_map/reshape | solution.py:422
  68.9 1.9 %copy.26 = bf16[2,32,16,256]{3,2,1,0:T(8,128)(2,1)} copy(bf16[2,32,16,256]{3,2,1,0:T(8,128)(2,1)} %get-tuple-element.13) | data formatting | bytes 1048576
  (2 shorter events, 0.0 us)
Async XLA Ops:
  1.7 14.2 %collective-permute-start = (bf16[4,128,512]{2,1,0:T(8,128)(2,1)S(1)}, bf16[4,128,512]{2,1,0:T(8,128)(2,1)S(1)}, u32[]{:S(2)}, u32[]{:S(2)}) collective-permute-start(bf16[4,128,512]{2,1,0:T(8,128)(2,1)S(1)} %bitcast.19), channel_id=1, source_target_pairs={{0,2},{1,3},{2,0},{3,1},{4,6},{5,7},{6,4},{7,5},{8,10},{9,11},{10,... | collective-permute-start | bytes 1572872 | tf_op jit(solution)/shard_map/ppermute | solution.py:375
  15.9 1.3 %copy-start = (bf16[4,128,512]{2,1,0:T(8,128)(2,1)}, bf16[4,128,512]{2,1,0:T(8,128)(2,1)S(1)}, u32[]{:S(2)}) copy-start(bf16[4,128,512]{2,1,0:T(8,128)(2,1)S(1)} %collective-permute-done.x0_ref) | copy-start | bytes 1572868

commit v4 on v3

--- a/solution.py
+++ b/solution.py
@@ -412,7 +412,7 @@
         ]
         + [dma((6,))] * 11,
         compiler_params=pltpu.CompilerParams(
-            collective_id=0, has_side_effects=True, vmem_limit_bytes=57 * 1024 * 1024
+            collective_id=0, has_side_effects=True, vmem_limit_bytes=50 * 1024 * 1024
         ),
         cost_estimate=pl.CostEstimate(
             flops=2 * RUNS * rows * 4 * feats * 512, bytes_accessed=16 * 1024 * 1024, transcendentals=0

time: 71.1 us -> 65.1 us (0.916)
  local copies, waits for them, and re-layouts: 18 us -> 13.5 us
  Pallas kernels: 49.9 us -> 48.6 us
    pallas_call x1, Pallas kernels: 49.9 us -> 48.6 us  [per_device_routed(): pl.pallas_call(functools.partial(routed_kernel, HEAD), out_shape=(jax.Sha...]
    transpose x1, local copies, waits for them, and re-layouts: 1 us -> 0.06 us  [per_device_routed(): out = out.reshape(2, 4, run, STEPS, QPK, HD).transpose(1, 2, 3, 0, 4, 5)]
    unnamed x5 -> x11, local copies, waits for them, and re-layouts: 10.3 us -> 9.41 us
  transfers between devices with their start and end apart: 1 -> 1, of which waited for: 0 -> 1; matrix products, arithmetic and copies ran while one was open for 18% -> 17% of each run, Pallas kernels for 0% -> 0%
where the time goes in v4:
time: 65.1 us; the launch traced here: 64.8 us
  Pallas kernels  48.6 us (75%)
  local copies, waits for them, and re-layouts  13.5 us (21%)
  starting transfers between devices  1.28 us (2%)
  between operations  0.75 us (1%)
    pallas_call x1, Pallas kernels, per_device_routed(): pl.pallas_call(functools.partial(routed_kernel, HEAD), out_shape=(jax.Sha...  48.6 us
    unnamed x11, local copies, waits for them, and re-layouts  9.41 us
  transfers between devices with their start and end apart: 1, of which 1 were waited for; matrix products, arithmetic and copies ran while one was open for 17% of the time, Pallas kernels for 0%

profile of v4, /device:TPU:9, one launch (start us, length us, event | category | flops | bytes accessed | tf_op | source)
XLA Modules:
  0.0 64.8 jit_solution(6760351104040913711)
XLA Ops:
  0.6 1.1 %slice.3 = bf16[16,32,512]{2,1,0:T(8,128)(2,1)S(1)} slice(bf16[16,32,2048]{2,1,0:T(8,128)(2,1)} %param.8), slice={[0:16], [0:32], [0:512]} | slice | bytes 1048576 | tf_op jit(solution)/shard_map/slice | solution.py:376
  1.7 1.3 %collective-permute-start = (bf16[4,128,512]{2,1,0:T(8,128)(2,1)S(1)}, bf16[4,128,512]{2,1,0:T(8,128)(2,1)S(1)}, u32[]{:S(2)}, u32[]{:S(2)}) collective-permute-start(bf16[4,128,512]{2,1,0:T(8,128)(2,1)S(1)} %bitcast.25), channel_id=1, source_target_pairs={{0,2},{1,3},{2,0},{3,1},{4,6},{5,7},{6,4},{7,5},{8,10},{9,11},{10,... | collective-permute-start | bytes 1572872 | tf_op jit(solution)/shard_map/ppermute | solution.py:375
  3.0 0.8 %copy.21 = s32[16,2]{1,0:T(8,128)S(1)} copy(s32[16,2]{0,1:T(2,128)} %param.15) | data formatting | bytes 256 | tf_op args[7]
  3.8 0.1 eq.15
  3.8 0.9 %reshape.56 = bf16[4,4,4,2,2,128]{5,4,3,2,1,0:T(2,128)(2,1)S(1)} reshape(bf16[16,4,2,256]{3,2,1,0:T(2,128)(2,1)} %param.14) | data formatting | bytes 131072 | tf_op jit(solution)/shard_map/reshape | solution.py:393
  4.8 1.1 %reshape.54 = bf16[4,4,4,2,8,128]{5,4,3,2,1,0:T(8,128)(2,1)S(1)} reshape(bf16[16,4,2048]{2,1,0:T(4,128)(2,1)} %param.13) | data formatting | bytes 524288 | tf_op jit(solution)/shard_map/reshape | solution.py:392
  5.9 0.0 copy-start
  6.0 0.0 copy-start.1
  6.0 0.0 copy-start.2
  6.0 0.0 copy-start.3
  6.0 7.8 %copy.20 = bf16[8192,2,256]{2,0,1:T(8,128)(2,1)} copy(bf16[8192,2,256]{2,1,0:T(2,128)(2,1)} %param.9) | data formatting | bytes 16777216 | tf_op args[1]
  13.8 0.1 select_reduce_fusion.inv_ref
  13.9 0.1 fusion
  14.1 0.1 pad_maximum_fusion
  14.2 0.4 collective-permute-done.x0_ref
  14.6 0.0 copy-done
  14.6 0.0 copy-done.1
  14.6 0.0 copy-done.2
  14.6 0.0 copy-done.3
  14.6 48.6 %shard_map.95 = (bf16[2,32,16,256]{3,2,1,0:T(8,128)(2,1)S(1)}, bf16[2,4,128,128]{3,2,1,0:T(8,128)(2,1)S(1)}) custom-call(bf16[4,128,2048]{2,1,0:T(8,128)(2,1)S(1)} %bitcast.20, bf16[4,128,512]{2,1,0:T(8,128)(2,1)S(1)} %collective-permute-done.x0_ref, bf16[2,4,2048,256]{3,2,1,0:T(8,128)(2,1)} %bitcast.24, bf16[2,256]{1,0:T(2,128)(2,1)S(1)} %copy-done.1, ...), custom_call_target="tpu_custom_call" | custom-call | flops 4294967296 | bytes 16777216 | tf_op jit(solution)/shard_map/pallas_call | solution.py:399
  63.2 0.1 copy.24
  63.3 0.8 %reshape.59 = bf16[16,4,2048]{2,1,0:T(4,128)(2,1)} reshape(bf16[4,4,4,2,8,128]{5,4,3,2,1,0:T(8,128)(2,1)S(1)} %copy.24) | data formatting | bytes 524288 | tf_op jit(solution)/shard_map/reshape | solution.py:422
  64.0 0.8 %copy.26 = bf16[2,32,16,256]{3,2,1,0:T(8,128)(2,1)} copy(bf16[2,32,16,256]{3,2,1,0:T(8,128)(2,1)S(1)} %get-tuple-element.13) | data formatting | bytes 1048576
  (6 shorter events, 0.1 us)
Async XLA Ops:
  1.7 12.9 %collective-permute-start = (bf16[4,128,512]{2,1,0:T(8,128)(2,1)S(1)}, bf16[4,128,512]{2,1,0:T(8,128)(2,1)S(1)}, u32[]{:S(2)}, u32[]{:S(2)}) collective-permute-start(bf16[4,128,512]{2,1,0:T(8,128)(2,1)S(1)} %bitcast.25), channel_id=1, source_target_pairs={{0,2},{1,3},{2,0},{3,1},{4,6},{5,7},{6,4},{7,5},{8,10},{9,11},{10,... | collective-permute-start | bytes 1572872 | tf_op jit(solution)/shard_map/ppermute | solution.py:375
  5.9 8.6 %copy-start = (bf16[16,32,2048]{2,1,0:T(8,128)(2,1)S(1)}, bf16[16,32,2048]{2,1,0:T(8,128)(2,1)}, u32[]{:S(2)}) copy-start(bf16[16,32,2048]{2,1,0:T(8,128)(2,1)} %param.8) | copy-start | bytes 6291460
  6.0 8.6 %copy-start.1 = (bf16[2,256]{1,0:T(2,128)(2,1)S(1)}, bf16[2,256]{1,0:T(2,128)(2,1)}, u32[]{:S(2)}) copy-start(bf16[2,256]{1,0:T(2,128)(2,1)} %bias_ref.1) | copy-start | bytes 3076
  6.0 8.6 %copy-start.2 = (s32[64]{0:T(128)S(1)}, s32[64]{0:T(128)}, u32[]{:S(2)}) copy-start(s32[64]{0:T(128)} %owner_ref.1) | copy-start | bytes 772
  6.0 8.6 %copy-start.3 = (s32[64]{0:T(128)S(1)}, s32[64]{0:T(128)}, u32[]{:S(2)}) copy-start(s32[64]{0:T(128)} %len_ref.1) | copy-start | bytes 772

commit v5 on v4

--- a/solution.py
+++ b/solution.py
@@ -190,8 +190,12 @@
         return remote(slot, slot, send, recv, where)
 
     cut_a, cut_b = rest // 2, rest // 3
-    cuts = [[(j, head, rest)] for j in range(RUNS - 1)]
-    cuts.append([(3, head, cut_a), (4, head + cut_a, cut_b), (5, head + cut_a + cut_b, rest - cut_a - cut_b)])
+    cuts = [
+        [(0, head, cut_b), (1, head + cut_b, rest - cut_b)],
+        [(2, head, rest)],
+        [(3, head, rest)],
+        [(4, head, cut_a), (5, head + cut_a, cut_b), (6, head + cut_a + cut_b, rest - cut_a - cut_b)],
+    ]
     x_copies = [
         [
             same(
@@ -204,6 +208,7 @@
         ]
         for j in range(RUNS)
     ]
+    pieces = [copy for copies in x_copies for copy in copies]
     sib_copies = [
         same(gathered.at[j, me], sib_send.at[j], sib_recv.at[j], {"tensor": sib}) for j in range(RUNS)
     ]
@@ -228,8 +233,8 @@
     gathered[0, me] = h_ref[runs[0]]
     pl.semaphore_wait(barrier, 5)
     x_copies[0][0].start()
+    x_copies[0][1].start()
     gathered[1, me] = h_ref[runs[1]]
-    x_copies[1][0].start()
     w_copies[0].start()
     w_copies[1].start()
     sib_copies[0].start()
@@ -318,9 +323,8 @@
         for at, (_, first, width) in enumerate(cuts[j]):
             x_copies[j][at].wait_recv()
             fwd_copies[j][at].start()
-            if j + 2 < RUNS:
-                for copy in x_copies[j + 2]:
-                    copy.start()
+            if cuts[j][at][0] + 2 < len(pieces):
+                pieces[cuts[j][at][0] + 2].start()
             k_one, v_one = half(j, across, first, width)
             k_acc, v_acc = k_acc + k_one, v_acc + v_one
             fwd_copies[j][at].wait_recv()
@@ -410,7 +414,7 @@
             pltpu.VMEM((count, BLK, 512), jnp.bfloat16),
             pltpu.VMEM((RUNS - 1, 8, BLK, 512), jnp.bfloat16),
         ]
-        + [dma((6,))] * 11,
+        + [dma((7,))] * 11,
         compiler_params=pltpu.CompilerParams(
             collective_id=0, has_side_effects=True, vmem_limit_bytes=50 * 1024 * 1024
         ),

time: 65.1 us -> 66 us (1.014)
  Pallas kernels: 48.6 us -> 49.5 us
    pallas_call x1, Pallas kernels: 48.6 us -> 49.5 us  [per_device_routed(): pl.pallas_call(functools.partial(routed_kernel, HEAD), out_shape=(jax.Sha...]
where the time goes in v5:
time: 66 us; the launch traced here: 65.8 us
  Pallas kernels  49.5 us (75%)
  local copies, waits for them, and re-layouts  13.5 us (20%)
  starting transfers between devices  1.28 us (2%)
  between operations  0.75 us (1%)
    pallas_call x1, Pallas kernels, per_device_routed(): pl.pallas_call(functools.partial(routed_kernel, HEAD), out_shape=(jax.Sha...  49.5 us
    unnamed x11, local copies, waits for them, and re-layouts  9.41 us
  transfers between devices with their start and end apart: 1, of which 1 were waited for; matrix products, arithmetic and copies ran while one was open for 17% of the time, Pallas kernels for 0%

profile of v5, /device:TPU:9, one launch (start us, length us, event | category | flops | bytes accessed | tf_op | source)
XLA Modules:
  0.0 65.8 jit_solution(13778342032592414623)
XLA Ops:
  0.6 1.1 %slice.3 = bf16[16,32,512]{2,1,0:T(8,128)(2,1)S(1)} slice(bf16[16,32,2048]{2,1,0:T(8,128)(2,1)} %param.8), slice={[0:16], [0:32], [0:512]} | slice | bytes 1048576 | tf_op jit(solution)/shard_map/slice | solution.py:380
  1.7 1.3 %collective-permute-start = (bf16[4,128,512]{2,1,0:T(8,128)(2,1)S(1)}, bf16[4,128,512]{2,1,0:T(8,128)(2,1)S(1)}, u32[]{:S(2)}, u32[]{:S(2)}) collective-permute-start(bf16[4,128,512]{2,1,0:T(8,128)(2,1)S(1)} %bitcast.25), channel_id=1, source_target_pairs={{0,2},{1,3},{2,0},{3,1},{4,6},{5,7},{6,4},{7,5},{8,10},{9,11},{10,... | collective-permute-start | bytes 1572872 | tf_op jit(solution)/shard_map/ppermute | solution.py:379
  3.0 0.8 %copy.21 = s32[16,2]{1,0:T(8,128)S(1)} copy(s32[16,2]{0,1:T(2,128)} %param.15) | data formatting | bytes 256 | tf_op args[7]
  3.8 0.1 eq.15
  3.8 0.9 %reshape.56 = bf16[4,4,4,2,2,128]{5,4,3,2,1,0:T(2,128)(2,1)S(1)} reshape(bf16[16,4,2,256]{3,2,1,0:T(2,128)(2,1)} %param.14) | data formatting | bytes 131072 | tf_op jit(solution)/shard_map/reshape | solution.py:397
  4.8 1.1 %reshape.54 = bf16[4,4,4,2,8,128]{5,4,3,2,1,0:T(8,128)(2,1)S(1)} reshape(bf16[16,4,2048]{2,1,0:T(4,128)(2,1)} %param.13) | data formatting | bytes 524288 | tf_op jit(solution)/shard_map/reshape | solution.py:396
  5.9 0.0 copy-start
  6.0 0.0 copy-start.1
  6.0 0.0 copy-start.2
  6.0 0.0 copy-start.3
  6.0 7.8 %copy.20 = bf16[8192,2,256]{2,0,1:T(8,128)(2,1)} copy(bf16[8192,2,256]{2,1,0:T(2,128)(2,1)} %param.9) | data formatting | bytes 16777216 | tf_op args[1]
  13.8 0.1 select_reduce_fusion.inv_ref
  13.9 0.1 fusion
  14.1 0.1 pad_maximum_fusion
  14.2 0.4 collective-permute-done.x0_ref
  14.6 0.0 copy-done
  14.6 0.0 copy-done.1
  14.6 0.0 copy-done.2
  14.6 0.0 copy-done.3
  14.6 49.5 %shard_map.95 = (bf16[2,32,16,256]{3,2,1,0:T(8,128)(2,1)S(1)}, bf16[2,4,128,128]{3,2,1,0:T(8,128)(2,1)S(1)}) custom-call(bf16[4,128,2048]{2,1,0:T(8,128)(2,1)S(1)} %bitcast.20, bf16[4,128,512]{2,1,0:T(8,128)(2,1)S(1)} %collective-permute-done.x0_ref, bf16[2,4,2048,256]{3,2,1,0:T(8,128)(2,1)} %bitcast.24, bf16[2,256]{1,0:T(2,128)(2,1)S(1)} %copy-done.1, ...), custom_call_target="tpu_custom_call" | custom-call | flops 4294967296 | bytes 16777216 | tf_op jit(solution)/shard_map/pallas_call | solution.py:403
  64.1 0.1 copy.24
  64.2 0.8 %reshape.59 = bf16[16,4,2048]{2,1,0:T(4,128)(2,1)} reshape(bf16[4,4,4,2,8,128]{5,4,3,2,1,0:T(8,128)(2,1)S(1)} %copy.24) | data formatting | bytes 524288 | tf_op jit(solution)/shard_map/reshape | solution.py:426
  65.0 0.8 %copy.26 = bf16[2,32,16,256]{3,2,1,0:T(8,128)(2,1)} copy(bf16[2,32,16,256]{3,2,1,0:T(8,128)(2,1)S(1)} %get-tuple-element.13) | data formatting | bytes 1048576
  (6 shorter events, 0.1 us)
Async XLA Ops:
  1.7 12.9 %collective-permute-start = (bf16[4,128,512]{2,1,0:T(8,128)(2,1)S(1)}, bf16[4,128,512]{2,1,0:T(8,128)(2,1)S(1)}, u32[]{:S(2)}, u32[]{:S(2)}) collective-permute-start(bf16[4,128,512]{2,1,0:T(8,128)(2,1)S(1)} %bitcast.25), channel_id=1, source_target_pairs={{0,2},{1,3},{2,0},{3,1},{4,6},{5,7},{6,4},{7,5},{8,10},{9,11},{10,... | collective-permute-start | bytes 1572872 | tf_op jit(solution)/shard_map/ppermute | solution.py:379
  5.9 8.6 %copy-start = (bf16[16,32,2048]{2,1,0:T(8,128)(2,1)S(1)}, bf16[16,32,2048]{2,1,0:T(8,128)(2,1)}, u32[]{:S(2)}) copy-start(bf16[16,32,2048]{2,1,0:T(8,128)(2,1)} %param.8) | copy-start | bytes 6291460
  6.0 8.6 %copy-start.1 = (bf16[2,256]{1,0:T(2,128)(2,1)S(1)}, bf16[2,256]{1,0:T(2,128)(2,1)}, u32[]{:S(2)}) copy-start(bf16[2,256]{1,0:T(2,128)(2,1)} %bias_ref.1) | copy-start | bytes 3076
  6.0 8.6 %copy-start.2 = (s32[64]{0:T(128)S(1)}, s32[64]{0:T(128)}, u32[]{:S(2)}) copy-start(s32[64]{0:T(128)} %owner_ref.1) | copy-start | bytes 772
  6.0 8.6 %copy-start.3 = (s32[64]{0:T(128)S(1)}, s32[64]{0:T(128)}, u32[]{:S(2)}) copy-start(s32[64]{0:T(128)} %len_ref.1) | copy-start | bytes 772

commit v6 on v2

--- a/solution.py
+++ b/solution.py
@@ -388,7 +388,7 @@
         ]
         + [dma((4,))] * 11,
         compiler_params=pltpu.CompilerParams(
-            collective_id=0, has_side_effects=True, vmem_limit_bytes=40 * 1024 * 1024
+            collective_id=0, has_side_effects=True, vmem_limit_bytes=50 * 1024 * 1024
         ),
         cost_estimate=pl.CostEstimate(
             flops=2 * RUNS * rows * 4 * feats * 512, bytes_accessed=16 * 1024 * 1024, transcendentals=0

time: 66.2 us -> 62.8 us (0.949)
  local copies, waits for them, and re-layouts: 16.9 us -> 13.5 us
    unnamed x13 -> x11, local copies, waits for them, and re-layouts: 12.8 us -> 9.41 us
  transfers between devices with their start and end apart: 1 -> 1, of which waited for: 1 -> 1; matrix products, arithmetic and copies ran while one was open for 17% -> 18% of each run, Pallas kernels for 0% -> 0%
where the time goes in v6:
time: 62.8 us; the launch traced here: 62.6 us
  Pallas kernels  46.3 us (74%)
  local copies, waits for them, and re-layouts  13.5 us (21%)
  starting transfers between devices  1.28 us (2%)
  between operations  0.75 us (1%)
    pallas_call x1, Pallas kernels, per_device_routed(): pl.pallas_call(functools.partial(routed_kernel, HEAD), out_shape=(jax.Sha...  46.3 us
    unnamed x11, local copies, waits for them, and re-layouts  9.41 us
    ppermute x1, starting transfers between devices, per_device_routed(): lax.ppermute(hidden[:, :, :HEAD].reshape(RUNS, rows, HEAD), 'tensor', [(t...  1.28 us
  transfers between devices with their start and end apart: 1, of which 1 were waited for; matrix products, arithmetic and copies ran while one was open for 18% of the time, Pallas kernels for 0%

profile of v6, /device:TPU:9, one launch (start us, length us, event | category | flops | bytes accessed | tf_op | source)
XLA Modules:
  0.0 62.6 jit_solution(7646541190655135431)
XLA Ops:
  0.6 1.1 %slice.3 = bf16[16,32,512]{2,1,0:T(8,128)(2,1)S(1)} slice(bf16[16,32,2048]{2,1,0:T(8,128)(2,1)} %param.8), slice={[0:16], [0:32], [0:512]} | slice | bytes 1048576 | tf_op jit(solution)/shard_map/slice | solution.py:352
  1.7 1.3 %collective-permute-start = (bf16[4,128,512]{2,1,0:T(8,128)(2,1)S(1)}, bf16[4,128,512]{2,1,0:T(8,128)(2,1)S(1)}, u32[]{:S(2)}, u32[]{:S(2)}) collective-permute-start(bf16[4,128,512]{2,1,0:T(8,128)(2,1)S(1)} %bitcast.25), channel_id=1, source_target_pairs={{0,2},{1,3},{2,0},{3,1},{4,6},{5,7},{6,4},{7,5},{8,10},{9,11},{10,... | collective-permute-start | bytes 1572872 | tf_op jit(solution)/shard_map/ppermute | solution.py:351
  3.0 0.8 %copy.21 = s32[16,2]{1,0:T(8,128)S(1)} copy(s32[16,2]{0,1:T(2,128)} %param.15) | data formatting | bytes 256 | tf_op args[7]
  3.8 0.1 eq.15
  3.8 0.9 %reshape.56 = bf16[4,4,4,2,2,128]{5,4,3,2,1,0:T(2,128)(2,1)S(1)} reshape(bf16[16,4,2,256]{3,2,1,0:T(2,128)(2,1)} %param.14) | data formatting | bytes 131072 | tf_op jit(solution)/shard_map/reshape | solution.py:369
  4.8 1.1 %reshape.54 = bf16[4,4,4,2,8,128]{5,4,3,2,1,0:T(8,128)(2,1)S(1)} reshape(bf16[16,4,2048]{2,1,0:T(4,128)(2,1)} %param.13) | data formatting | bytes 524288 | tf_op jit(solution)/shard_map/reshape | solution.py:368
  5.9 0.0 copy-start
  6.0 0.0 copy-start.1
  6.0 0.0 copy-start.2
  6.0 0.0 copy-start.3
  6.0 7.8 %copy.20 = bf16[8192,2,256]{2,0,1:T(8,128)(2,1)} copy(bf16[8192,2,256]{2,1,0:T(2,128)(2,1)} %param.9) | data formatting | bytes 16777216 | tf_op args[1]
  13.8 0.1 select_reduce_fusion.inv_ref
  13.9 0.1 fusion
  14.1 0.1 pad_maximum_fusion
  14.2 0.4 collective-permute-done.x0_ref
  14.6 0.0 copy-done
  14.6 0.0 copy-done.1
  14.6 0.0 copy-done.2
  14.6 0.0 copy-done.3
  14.6 46.3 %shard_map.95 = (bf16[2,32,16,256]{3,2,1,0:T(8,128)(2,1)S(1)}, bf16[2,4,128,128]{3,2,1,0:T(8,128)(2,1)S(1)}) custom-call(bf16[4,128,2048]{2,1,0:T(8,128)(2,1)S(1)} %bitcast.20, bf16[4,128,512]{2,1,0:T(8,128)(2,1)S(1)} %collective-permute-done.x0_ref, bf16[2,4,2048,256]{3,2,1,0:T(8,128)(2,1)} %bitcast.24, bf16[2,256]{1,0:T(2,128)(2,1)S(1)} %copy-done.1, ...), custom_call_target="tpu_custom_call" | custom-call | flops 4294967296 | bytes 16777216 | tf_op jit(solution)/shard_map/pallas_call | solution.py:375
  60.9 0.1 copy.24
  61.0 0.8 %reshape.59 = bf16[16,4,2048]{2,1,0:T(4,128)(2,1)} reshape(bf16[4,4,4,2,8,128]{5,4,3,2,1,0:T(8,128)(2,1)S(1)} %copy.24) | data formatting | bytes 524288 | tf_op jit(solution)/shard_map/reshape | solution.py:398
  61.8 0.8 %copy.26 = bf16[2,32,16,256]{3,2,1,0:T(8,128)(2,1)} copy(bf16[2,32,16,256]{3,2,1,0:T(8,128)(2,1)S(1)} %get-tuple-element.13) | data formatting | bytes 1048576
  (6 shorter events, 0.1 us)
Async XLA Ops:
  1.7 12.9 %collective-permute-start = (bf16[4,128,512]{2,1,0:T(8,128)(2,1)S(1)}, bf16[4,128,512]{2,1,0:T(8,128)(2,1)S(1)}, u32[]{:S(2)}, u32[]{:S(2)}) collective-permute-start(bf16[4,128,512]{2,1,0:T(8,128)(2,1)S(1)} %bitcast.25), channel_id=1, source_target_pairs={{0,2},{1,3},{2,0},{3,1},{4,6},{5,7},{6,4},{7,5},{8,10},{9,11},{10,... | collective-permute-start | bytes 1572872 | tf_op jit(solution)/shard_map/ppermute | solution.py:351
  5.9 8.6 %copy-start = (bf16[16,32,2048]{2,1,0:T(8,128)(2,1)S(1)}, bf16[16,32,2048]{2,1,0:T(8,128)(2,1)}, u32[]{:S(2)}) copy-start(bf16[16,32,2048]{2,1,0:T(8,128)(2,1)} %param.8) | copy-start | bytes 6291460
  6.0 8.6 %copy-start.1 = (bf16[2,256]{1,0:T(2,128)(2,1)S(1)}, bf16[2,256]{1,0:T(2,128)(2,1)}, u32[]{:S(2)}) copy-start(bf16[2,256]{1,0:T(2,128)(2,1)} %bias_ref.1) | copy-start | bytes 3076
  6.0 8.6 %copy-start.2 = (s32[64]{0:T(128)S(1)}, s32[64]{0:T(128)}, u32[]{:S(2)}) copy-start(s32[64]{0:T(128)} %owner_ref.1) | copy-start | bytes 772
  6.0 8.6 %copy-start.3 = (s32[64]{0:T(128)S(1)}, s32[64]{0:T(128)}, u32[]{:S(2)}) copy-start(s32[64]{0:T(128)} %len_ref.1) | copy-start | bytes 772
